TPU v7x, 512 devices: a whole 4x4x16 slice. The times are simulated.
512 devices in a mesh: rows: 128 (over z, x, core), batch: 4 (over y).
Axes of the slice: x: 4, y: 4, z: 16, core: 2. Of those that a mesh axis runs over, the one named last changes fastest.
Arguments:
- pixels: float32 [48, 256, 512], P('batch', 'rows'), parts along dimension 0, may hold values from -8 to 8
- probes: int32 [48, 256, 512], P('batch', 'rows'), parts along dimension 0, may hold values from 0 to 1
- in_weight: bfloat16 [3, 3, 12, 512], replicated, may hold values from -0.625 to 0.625
- in_bias: float32 [512], replicated, may hold values from -3 to 3
- in_beta: float32 [512], replicated, may hold values from 0.5 to 4
- mid_weight: bfloat16 [512, 512], replicated, may hold values from -0.25 to 0.25
- mid_bias: float32 [512], replicated, may hold values from -3 to 3
- mid_beta: float32 [512], replicated, may hold values from 0.5 to 4
- out_weight: bfloat16 [3, 3, 12, 512], replicated, may hold values from -0.5 to 0.5
- out_bias: float32 [12], replicated, may hold values from -3 to 3
Outputs:
- latent: float32 [48, 256, 512], P('batch', 'rows'), parts along dimension 0
- bits_map: float32 [1024, 512], P(('batch', 'rows')), parts along dimension 0
- bits_mean: float32 [4], P('batch'), parts along dimension 0
There are 4 independent parts, one for each index of `batch`. A program takes and returns all parts, laid end to end along the dimension named above; an argument that names none is the same for every part. Nothing has to cross between parts.
All inputs are finite; a program needn't handle non-finite values.
Results may differ from a plain program's by a relative error of at most 0.0044.
Values may be sent and summed in bfloat16 or wider, within the bound.
A program may use at most 64 MiB of HBM per device.

v0:
```python
import math

import jax
import jax.numpy as jnp
from jax import lax
from jax.sharding import PartitionSpec as P

TERMS = 4


def extended_2(shard, sides, width):
    for axis, dim in sides:
        peers, length = (lax.axis_size(axis), shard.shape[dim])
        up = [(i, (i + 1) % peers) for i in range(peers - 1)]
        down = [(j, i) for i, j in up]
        last = lax.slice_in_dim(shard, length - width, length, axis=dim)
        first = lax.slice_in_dim(shard, 0, width, axis=dim)
        before = lax.ppermute(last, axis, up)
        after = lax.ppermute(first, axis, down)
        shard = jnp.concatenate([before, shard, after], axis=dim)
    return shard


def activate(preact, gain_rate):
    gate_value = jax.nn.sigmoid(gain_rate * preact)
    return preact * gate_value / 1.1


def derivative(preact, gain_rate):
    gate_value = jax.nn.sigmoid(gain_rate * preact)
    return (gate_value + gain_rate * preact * gate_value * (1.0 - gate_value)) / 1.1


def expand(extended):
    height = extended.shape[1] - 2
    breadth = extended.shape[2]
    padded = jnp.pad(extended, ((0, 0), (0, 0), (1, 1)))
    pieces = [
        padded[:, row_off : row_off + height, col_off : col_off + breadth]
        for row_off in range(3)
        for col_off in range(3)
    ]
    return jnp.stack(pieces).reshape(9 * extended.shape[0], height * breadth)


def contract_first(matrix, columns):
    return lax.dot_general(
        matrix, columns, (((0,), (0,)), ((), ())), preferred_element_type=jnp.float32
    )


def column_taps(kernel, preact):
    channels = kernel.shape[2]
    height = preact.shape[1]
    breadth = preact.shape[2]
    products = jnp.dot(
        kernel.reshape(9 * channels, kernel.shape[3]),
        preact.reshape(preact.shape[0], height * breadth),
        preferred_element_type=jnp.float32,
    )
    tap_grid = products.reshape(3, 3, channels, height, breadth)
    left_taps = jnp.pad(tap_grid[:, 0, :, :, :-1], ((0, 0), (0, 0), (0, 0), (1, 0)))
    right_taps = jnp.pad(tap_grid[:, 2, :, :, 1:], ((0, 0), (0, 0), (0, 0), (0, 1)))
    return left_taps + tap_grid[:, 1] + right_taps


def spread(kernel, preact):
    extended = extended_2(preact, (("rows", 1),), 1)
    tap_sums = column_taps(kernel, extended)
    return tap_sums[0, :, :-2] + tap_sums[1, :, 1:-1] + tap_sums[2, :, 2:]


def per_device(
    pixels,
    probes,
    in_weight,
    in_bias,
    in_beta,
    mid_weight,
    mid_bias,
    mid_beta,
    out_weight,
    out_bias,
):
    channels, height, breadth = pixels.shape
    hidden_width = in_weight.shape[3]
    in_rate = in_beta[:, None]
    mid_rate = mid_beta[:, None]
    extended = extended_2(pixels.astype(jnp.bfloat16), (("rows", 1),), 1)
    first_pre = (
        contract_first(in_weight.reshape(9 * channels, hidden_width), expand(extended))
        + in_bias[:, None]
    )
    first_act = activate(first_pre, in_rate).astype(jnp.bfloat16)
    second = contract_first(mid_weight, first_act) + mid_bias[:, None]
    second_act = activate(second, mid_rate).astype(jnp.bfloat16)
    in_slope = derivative(first_pre, in_rate)
    mid_slope = derivative(second, mid_rate)
    branch = spread(out_weight, second_act.reshape(hidden_width, height, breadth))
    latent = pixels + (branch + out_bias[:, None, None])
    sign_field = (2 * probes - 1).astype(jnp.float32)
    flip_out = out_weight[::-1, ::-1].reshape(9 * channels, hidden_width)
    flip_in = in_weight[::-1, ::-1]
    vector = sign_field
    logdet = jnp.zeros((height, breadth), jnp.float32)
    for term_index in range(1, TERMS + 1):
        rimmed = extended_2(vector.astype(jnp.bfloat16), (("rows", 1),), 1)
        back_out = contract_first(flip_out, expand(rimmed))
        back_mid = (back_out * mid_slope).astype(jnp.bfloat16)
        back_in = jnp.dot(mid_weight, back_mid, preferred_element_type=jnp.float32)
        back_first = (back_in * in_slope).astype(jnp.bfloat16)
        vector = spread(flip_in, back_first.reshape(hidden_width, height, breadth))
        logdet = logdet + (-1.0) ** (term_index + 1) / term_index * jnp.sum(
            vector * sign_field, axis=0
        )
    log_prior = -0.5 * jnp.sum(latent * latent, axis=0) - 0.5 * channels * math.log(2.0 * math.pi)
    bits_map = 8.0 - (log_prior + logdet) / (channels * math.log(2.0))
    overall = lax.psum(jnp.sum(bits_map), "rows")
    bits_mean = (overall / (height * lax.axis_size("rows") * breadth)).reshape(1)
    return (latent, bits_map, bits_mean)


def solution(mesh):
    placed = (
        P("batch", "rows", None),
        P("batch", "rows", None),
        P(),
        P(),
        P(),
        P(),
        P(),
        P(),
        P(),
        P(),
    )
    return jax.shard_map(
        per_device,
        mesh=mesh,
        in_specs=placed,
        out_specs=(P("batch", "rows", None), P(("batch", "rows"), None), P("batch")),
        check_vma=False,
    )
```

profile of v0, /device:TPU:392, one launch (start us, length us, event | category | flops | bytes accessed | tf_op | source)
XLA Modules:
  0.0 421.6 jit_solution(6086087168230883625)
XLA Ops:
  0.7 0.9 convert_element_type.75
  1.6 1.9 collective-permute-start
  3.5 7.0 %collective-permute-start.1 = (bf16[12,1,512]{2,1,0:T(2,128)(2,1)S(1)}, bf16[12,1,512]{2,1,0:T(2,128)(2,1)S(1)}, u32[]{:S(2)}, u32[]{:S(2)}) collective-permute-start(bf16[12,1,512]{2,1,0:T(2,128)(2,1)S(1)} %get-tuple-element.46), channel_id=1, source_target_pairs={{4,0},{8,4},{12,8},{16,12},{20,16},{24,20},{28,24},{32,28},{36,32}... | collective-permute-start | bytes 36872 | tf_op jit(solution)/shard_map/ppermute | solution.py:19
  10.5 0.8 convert_convert_fusion
  11.4 1.9 collective-permute-start.4
  13.3 7.0 %collective-permute-start.5 = (bf16[12,1,512]{2,1,0:T(2,128)(2,1)S(1)}, bf16[12,1,512]{2,1,0:T(2,128)(2,1)S(1)}, u32[]{:S(2)}, u32[]{:S(2)}) collective-permute-start(bf16[12,1,512]{2,1,0:T(2,128)(2,1)S(1)} %get-tuple-element.44), channel_id=1, source_target_pairs={{4,0},{8,4},{12,8},{16,12},{20,16},{24,20},{28,24},{32,28},{36,32}... | collective-permute-start | bytes 36872 | tf_op jit(solution)/shard_map/ppermute | solution.py:19
  20.3 0.9 reshape.100
  21.2 0.9 rev.6
  25.7 2.5 fusion.9
  28.2 4.7 %fusion.6 = bf16[512,1024]{0,1:T(8,128)(2,1)S(1)} fusion(bf16[512,512]{1,0:T(8,128)(2,1)S(1)} %copy-done, bf16[108,1024]{1,0:T(8,128)(2,1)S(1)} %bitcast.457, bf16[108,512]{1,0:T(8,128)(2,1)S(1)} %reshape.106, f32[1024,512]{1,0:T(8,128)} %get-tuple-element.48, f32[512]{0:T(512)S(1)} %copy-done.23, f32[512]{0:T(512)S(1)} %copy-done.25, ...), kind=kOutput, calls=%fused_computation.23 | convolution fusion | flops 662700032 | bytes 6107136 | tf_op jit(solution)/shard_map/dot_general | solution.py:110
  33.0 0.9 fusion.51
  33.8 1.9 collective-permute-start.6
  35.7 7.0 %collective-permute-start.7 = (bf16[512,1,512]{0,2,1:T(8,128)(2,1)S(1)}, bf16[512,1,512]{0,2,1:T(8,128)(2,1)}, u32[]{:S(2)}, u32[]{:S(2)}) collective-permute-start(bf16[512,1,512]{0,2,1:T(8,128)(2,1)S(1)} %get-tuple-element.24), channel_id=1, source_target_pairs={{4,0},{8,4},{12,8},{16,12},{20,16},{24,20},{28,24},{32,28},{36,32}... | collective-permute-start | bytes 1572872 | tf_op jit(solution)/shard_map/ppermute | solution.py:19
  42.8 5.2 %collective-permute-done.6 = bf16[512,1,512]{0,2,1:T(8,128)(2,1)} collective-permute-done((bf16[512,1,512]{0,2,1:T(8,128)(2,1)}, bf16[512,1,512]{0,2,1:T(8,128)(2,1)}, u32[]{:S(2)}, u32[]{:S(2)}) %collective-permute-start.6) | collective-permute-done | bytes 524320 | tf_op jit(solution)/shard_map/ppermute | solution.py:18
  48.0 1.4 collective-permute-done.7
  49.4 1.4 pad_maximum_fusion.1
  52.9 1.9 collective-permute-start.8
  54.8 7.2 %collective-permute-start.9 = (bf16[12,1,512]{2,1,0:T(2,128)(2,1)S(1)}, bf16[12,1,512]{2,1,0:T(2,128)(2,1)S(1)}, u32[]{:S(2)}, u32[]{:S(2)}) collective-permute-start(bf16[12,1,512]{2,1,0:T(2,128)(2,1)S(1)} %get-tuple-element.42), channel_id=1, source_target_pairs={{4,0},{8,4},{12,8},{16,12},{20,16},{24,20},{28,24},{32,28},{36,32}... | collective-permute-start | bytes 36872 | tf_op jit(solution)/shard_map/ppermute | solution.py:19
  62.1 1.5 collective-permute-done.9
  64.7 4.3 %fusion.4 = bf16[512,1024]{0,1:T(8,128)(2,1)S(1)} fusion(bf16[512,512]{1,0:T(8,128)(2,1)S(1)} %copy-done, bf16[108,1024]{1,0:T(8,128)(2,1)S(1)} %bitcast.459, bf16[108,512]{1,0:T(8,128)(2,1)S(1)} %copy-done.20, f32[1024,512]{1,0:T(8,128)} %get-tuple-element.48, f32[512]{0:T(512)S(1)} %copy-done.24, f32[512]{0:T(512)S(1)} %copy-done.26, ...), kind=kOutput, calls=%fused_computation.19 | convolution fusion | flops 662700032 | bytes 6107136 | tf_op jit(solution)/shard_map/dot_general | solution.py:110
  69.1 1.9 collective-permute-start.10
  71.0 7.1 %collective-permute-start.11 = (bf16[512,1,512]{0,2,1:T(8,128)(2,1)S(1)}, bf16[512,1,512]{0,2,1:T(8,128)(2,1)S(1)}, u32[]{:S(2)}, u32[]{:S(2)}) collective-permute-start(bf16[512,1,512]{0,2,1:T(8,128)(2,1)S(1)} %get-tuple-element.22), channel_id=1, source_target_pairs={{4,0},{8,4},{12,8},{16,12},{20,16},{24,20},{28,24},{32,28},{36,32}... | collective-permute-start | bytes 1572872 | tf_op jit(solution)/shard_map/ppermute | solution.py:19
  78.2 4.7 %collective-permute-done.10 = bf16[512,1,512]{0,2,1:T(8,128)(2,1)S(1)} collective-permute-done((bf16[512,1,512]{0,2,1:T(8,128)(2,1)S(1)}, bf16[512,1,512]{0,2,1:T(8,128)(2,1)S(1)}, u32[]{:S(2)}, u32[]{:S(2)}) %collective-permute-start.10) | collective-permute-done | bytes 524320 | tf_op jit(solution)/shard_map/ppermute | solution.py:18
  82.9 1.8 collective-permute-done.11
  86.9 1.9 collective-permute-start.12
  88.8 7.1 %collective-permute-start.13 = (bf16[12,1,512]{2,1,0:T(2,128)(2,1)S(1)}, bf16[12,1,512]{2,1,0:T(2,128)(2,1)S(1)}, u32[]{:S(2)}, u32[]{:S(2)}) collective-permute-start(bf16[12,1,512]{2,1,0:T(2,128)(2,1)S(1)} %get-tuple-element.40), channel_id=1, source_target_pairs={{4,0},{8,4},{12,8},{16,12},{20,16},{24,20},{28,24},{32,28},{36,32}... | collective-permute-start | bytes 36872 | tf_op jit(solution)/shard_map/ppermute | solution.py:19
  96.0 1.5 collective-permute-done.13
  98.5 4.3 %fusion.2 = bf16[512,1024]{0,1:T(8,128)(2,1)S(1)} fusion(bf16[512,512]{1,0:T(8,128)(2,1)S(1)} %copy-done, bf16[108,1024]{1,0:T(8,128)(2,1)S(1)} %bitcast.460, bf16[108,512]{1,0:T(8,128)(2,1)S(1)} %copy-done.21, f32[1024,512]{1,0:T(8,128)} %get-tuple-element.48, f32[512]{0:T(512)S(1)} %copy-done.24, f32[512]{0:T(512)S(1)} %copy-done.26, ...), kind=kOutput, calls=%fused_computation.15 | convolution fusion | flops 662700032 | bytes 6107136 | tf_op jit(solution)/shard_map/dot_general | solution.py:110
  102.9 1.0 fusion.49
  103.9 1.9 collective-permute-start.14
  105.8 7.0 %collective-permute-start.15 = (bf16[512,1,512]{0,2,1:T(8,128)(2,1)}, bf16[512,1,512]{0,2,1:T(8,128)(2,1)}, u32[]{:S(2)}, u32[]{:S(2)}) collective-permute-start(bf16[512,1,512]{0,2,1:T(8,128)(2,1)} %get-tuple-element.20), channel_id=1, source_target_pairs={{4,0},{8,4},{12,8},{16,12},{20,16},{24,20},{28,24},{32,28},{36,32}... | collective-permute-start | bytes 1572872 | tf_op jit(solution)/shard_map/ppermute | solution.py:19
  113.5 0.9 fusion.52
  114.4 1.9 collective-permute-start.2
  116.3 7.0 %collective-permute-start.3 = (bf16[512,1,512]{0,2,1:T(8,128)(2,1)S(1)}, bf16[512,1,512]{0,2,1:T(8,128)(2,1)}, u32[]{:S(2)}, u32[]{:S(2)}) collective-permute-start(bf16[512,1,512]{0,2,1:T(8,128)(2,1)S(1)} %get-tuple-element.26), channel_id=1, source_target_pairs={{4,0},{8,4},{12,8},{16,12},{20,16},{24,20},{28,24},{32,28},{36,32}... | collective-permute-start | bytes 1572872 | tf_op jit(solution)/shard_map/ppermute | solution.py:19
  123.3 1.4 pad_maximum_fusion.3
  126.7 1.9 collective-permute-start.16
  128.6 7.0 %collective-permute-start.17 = (bf16[12,1,512]{2,1,0:T(2,128)(2,1)S(1)}, bf16[12,1,512]{2,1,0:T(2,128)(2,1)S(1)}, u32[]{:S(2)}, u32[]{:S(2)}) collective-permute-start(bf16[12,1,512]{2,1,0:T(2,128)(2,1)S(1)} %get-tuple-element.38), channel_id=1, source_target_pairs={{4,0},{8,4},{12,8},{16,12},{20,16},{24,20},{28,24},{32,28},{36,32}... | collective-permute-start | bytes 36872 | tf_op jit(solution)/shard_map/ppermute | solution.py:19
  135.6 1.4 pad_maximum_fusion
  138.2 5.3 %fusion = bf16[512,1024]{0,1:T(8,128)(2,1)} fusion(bf16[512,512]{1,0:T(8,128)(2,1)S(1)} %copy-done, bf16[108,1024]{1,0:T(8,128)(2,1)S(1)} %bitcast.458, bf16[108,512]{1,0:T(8,128)(2,1)S(1)} %copy-done.21, f32[1024,512]{1,0:T(8,128)} %get-tuple-element.48, f32[512]{0:T(512)S(1)} %copy-done.24, f32[512]{0:T(512)S(1)} %copy-done.26, ...), kind=kOutput, calls=%fused_computation.11 | convolution fusion | flops 662700032 | bytes 6107136 | tf_op jit(solution)/shard_map/dot_general | solution.py:110
  143.5 2.3 fusion.48
  145.8 1.9 collective-permute-start.18
  147.7 7.2 %collective-permute-start.19 = (bf16[512,1,512]{0,2,1:T(8,128)(2,1)}, bf16[512,1,512]{0,2,1:T(8,128)(2,1)}, u32[]{:S(2)}, u32[]{:S(2)}) collective-permute-start(bf16[512,1,512]{0,2,1:T(8,128)(2,1)} %get-tuple-element.18), channel_id=1, source_target_pairs={{4,0},{8,4},{12,8},{16,12},{20,16},{24,20},{28,24},{32,28},{36,32}... | collective-permute-start | bytes 1572872 | tf_op jit(solution)/shard_map/ppermute | solution.py:19
  156.8 3.1 collective-permute-done.18
  159.9 1.8 collective-permute-done.19
  161.7 1.4 pad_maximum_fusion.4
  165.1 0.8 fusion.31
  165.9 1.2 fusion.46
  167.1 252.6 %psum.7 = f32[]{:T(128)} all-reduce(f32[]{:T(128)} %get-tuple-element.7), channel_id=1, replica_groups=mesh['rows'=128,'batch'=4] {'rows'}, use_global_device_ids=true, to_apply=%region_6.7 | all-reduce | flops 1 | bytes 8 | tf_op jit(solution)/shard_map/psum | solution.py:118
  (169 shorter events, 17.0 us)
Async XLA Ops:
  0.6 25.0 %copy-start = (bf16[512,512]{1,0:T(8,128)(2,1)S(1)}, bf16[512,512]{1,0:T(8,128)(2,1)}, u32[]{:S(2)}) copy-start(bf16[512,512]{1,0:T(8,128)(2,1)} %param.15) | copy-start | bytes 1572868
  0.6 23.9 %copy-start.10 = (s32[12,2,512]{2,1,0:T(2,128)S(1)}, s32[12,2,512]{2,1,0:T(2,128)}, u32[]{:S(2)}) copy-start(s32[12,2,512]{2,1,0:T(2,128)} %param.11) | copy-start | bytes 147460
  1.6 20.6 %collective-permute-start = (bf16[12,1,512]{2,1,0:T(2,128)(2,1)S(1)}, bf16[12,1,512]{2,1,0:T(2,128)(2,1)S(1)}, u32[]{:S(2)}, u32[]{:S(2)}) collective-permute-start(bf16[12,1,512]{2,1,0:T(2,128)(2,1)S(1)} %get-tuple-element.45), channel_id=1, source_target_pairs={{0,4},{4,8},{8,12},{12,16},{16,20},{20,24},{24,28},{28,32},{32,36}... | collective-permute-start | bytes 36872 | tf_op jit(solution)/shard_map/ppermute | solution.py:18
  3.5 18.7 %collective-permute-start.1 = (bf16[12,1,512]{2,1,0:T(2,128)(2,1)S(1)}, bf16[12,1,512]{2,1,0:T(2,128)(2,1)S(1)}, u32[]{:S(2)}, u32[]{:S(2)}) collective-permute-start(bf16[12,1,512]{2,1,0:T(2,128)(2,1)S(1)} %get-tuple-element.46), channel_id=1, source_target_pairs={{4,0},{8,4},{12,8},{16,12},{20,16},{24,20},{28,24},{32,28},{36,32}... | collective-permute-start | bytes 36872 | tf_op jit(solution)/shard_map/ppermute | solution.py:19
  11.4 12.7 %collective-permute-start.4 = (bf16[12,1,512]{2,1,0:T(2,128)(2,1)S(1)}, bf16[12,1,512]{2,1,0:T(2,128)(2,1)S(1)}, u32[]{:S(2)}, u32[]{:S(2)}) collective-permute-start(bf16[12,1,512]{2,1,0:T(2,128)(2,1)S(1)} %get-tuple-element.43), channel_id=1, source_target_pairs={{0,4},{4,8},{8,12},{12,16},{16,20},{20,24},{24,28},{28,32},{32,36}... | collective-permute-start | bytes 36872 | tf_op jit(solution)/shard_map/ppermute | solution.py:18
  13.3 10.8 %collective-permute-start.5 = (bf16[12,1,512]{2,1,0:T(2,128)(2,1)S(1)}, bf16[12,1,512]{2,1,0:T(2,128)(2,1)S(1)}, u32[]{:S(2)}, u32[]{:S(2)}) collective-permute-start(bf16[12,1,512]{2,1,0:T(2,128)(2,1)S(1)} %get-tuple-element.44), channel_id=1, source_target_pairs={{4,0},{8,4},{12,8},{16,12},{20,16},{24,20},{28,24},{32,28},{36,32}... | collective-permute-start | bytes 36872 | tf_op jit(solution)/shard_map/ppermute | solution.py:19
  22.2 6.1 %copy-start.19 = (bf16[108,512]{1,0:T(8,128)(2,1)}, bf16[108,512]{1,0:T(8,128)(2,1)S(1)}, u32[]{:S(2)}) copy-start(bf16[108,512]{1,0:T(8,128)(2,1)S(1)} %reshape.106) | copy-start | bytes 331780
  24.0 1.6 copy-start.23
  24.1 1.6 copy-start.25
  24.1 1.6 copy-start.27
  24.1 1.6 copy-start.29
  25.7 2.5 copy-start.6
  28.2 85.2 %copy-start.1 = (bf16[512,1024]{0,1:T(8,128)(2,1)}, bf16[512,1024]{0,1:T(8,128)(2,1)S(1)}, u32[]{:S(2)}) copy-start(bf16[512,1024]{0,1:T(8,128)(2,1)S(1)} %get-tuple-element.47) | copy-start | bytes 3145732
  32.9 9.8 %copy-start.7 = (bf16[3,3,12,512]{3,2,1,0:T(8,128)(2,1)S(1)}, bf16[3,3,12,512]{3,2,1,0:T(8,128)(2,1)}, u32[]{:S(2)}) copy-start(bf16[3,3,12,512]{3,2,1,0:T(8,128)(2,1)} %param.12) | copy-start | bytes 331780
  33.8 14.1 %collective-permute-start.6 = (bf16[512,1,512]{0,2,1:T(8,128)(2,1)}, bf16[512,1,512]{0,2,1:T(8,128)(2,1)}, u32[]{:S(2)}, u32[]{:S(2)}) collective-permute-start(bf16[512,1,512]{0,2,1:T(8,128)(2,1)} %get-tuple-element.23), channel_id=1, source_target_pairs={{0,4},{4,8},{8,12},{12,16},{16,20},{20,24},{24,28},{28,32},{32,36}... | collective-permute-start | bytes 1572872 | tf_op jit(solution)/shard_map/ppermute | solution.py:18
  35.7 13.6 %collective-permute-start.7 = (bf16[512,1,512]{0,2,1:T(8,128)(2,1)S(1)}, bf16[512,1,512]{0,2,1:T(8,128)(2,1)}, u32[]{:S(2)}, u32[]{:S(2)}) collective-permute-start(bf16[512,1,512]{0,2,1:T(8,128)(2,1)S(1)} %get-tuple-element.24), channel_id=1, source_target_pairs={{4,0},{8,4},{12,8},{16,12},{20,16},{24,20},{28,24},{32,28},{36,32}... | collective-permute-start | bytes 1572872 | tf_op jit(solution)/shard_map/ppermute | solution.py:19
  42.8 81.9 %copy-start.4 = (bf16[108,512]{1,0:T(8,128)(2,1)}, bf16[108,512]{1,0:T(8,128)(2,1)S(1)}, u32[]{:S(2)}) copy-start(bf16[108,512]{1,0:T(8,128)(2,1)S(1)} %reshape.109) | copy-start | bytes 331780
  52.2 12.4 %copy-start.20 = (bf16[108,512]{1,0:T(8,128)(2,1)S(1)}, bf16[108,512]{1,0:T(8,128)(2,1)}, u32[]{:S(2)}) copy-start(bf16[108,512]{1,0:T(8,128)(2,1)} %copy-done.19) | copy-start | bytes 331780
  52.2 12.4 %copy-start.24 = (f32[512]{0:T(512)S(1)}, f32[512]{0:T(512)}, u32[]{:S(2)}) copy-start(f32[512]{0:T(512)} %param.17) | copy-start | bytes 6148
  52.2 12.4 %copy-start.26 = (f32[512]{0:T(512)S(1)}, f32[512]{0:T(512)}, u32[]{:S(2)}) copy-start(f32[512]{0:T(512)} %param.16) | copy-start | bytes 6148
  52.3 12.4 %copy-start.28 = (f32[512]{0:T(512)S(1)}, f32[512]{0:T(512)}, u32[]{:S(2)}) copy-start(f32[512]{0:T(512)} %param.14) | copy-start | bytes 6148
  52.3 12.4 %copy-start.30 = (f32[512]{0:T(512)S(1)}, f32[512]{0:T(512)}, u32[]{:S(2)}) copy-start(f32[512]{0:T(512)} %param.13) | copy-start | bytes 6148
  52.8 11.6 %copy-start.13 = (f32[1,12,2,512]{3,2,1,0:T(2,128)}, f32[1,12,2,512]{3,2,1,0:T(2,128)S(1)}, u32[]{:S(2)}) copy-start(f32[1,12,2,512]{3,2,1,0:T(2,128)S(1)} %get-tuple-element.16) | copy-start | bytes 147460
  52.9 9.2 %collective-permute-start.8 = (bf16[12,1,512]{2,1,0:T(2,128)(2,1)S(1)}, bf16[12,1,512]{2,1,0:T(2,128)(2,1)S(1)}, u32[]{:S(2)}, u32[]{:S(2)}) collective-permute-start(bf16[12,1,512]{2,1,0:T(2,128)(2,1)S(1)} %get-tuple-element.41), channel_id=1, source_target_pairs={{0,4},{4,8},{8,12},{12,16},{16,20},{20,24},{24,28},{28,32},{32,36}... | collective-permute-start | bytes 36872 | tf_op jit(solution)/shard_map/ppermute | solution.py:18
  54.8 8.8 %collective-permute-start.9 = (bf16[12,1,512]{2,1,0:T(2,128)(2,1)S(1)}, bf16[12,1,512]{2,1,0:T(2,128)(2,1)S(1)}, u32[]{:S(2)}, u32[]{:S(2)}) collective-permute-start(bf16[12,1,512]{2,1,0:T(2,128)(2,1)S(1)} %get-tuple-element.42), channel_id=1, source_target_pairs={{4,0},{8,4},{12,8},{16,12},{20,16},{24,20},{28,24},{32,28},{36,32}... | collective-permute-start | bytes 36872 | tf_op jit(solution)/shard_map/ppermute | solution.py:19
  69.1 13.8 %collective-permute-start.10 = (bf16[512,1,512]{0,2,1:T(8,128)(2,1)S(1)}, bf16[512,1,512]{0,2,1:T(8,128)(2,1)S(1)}, u32[]{:S(2)}, u32[]{:S(2)}) collective-permute-start(bf16[512,1,512]{0,2,1:T(8,128)(2,1)S(1)} %get-tuple-element.21), channel_id=1, source_target_pairs={{0,4},{4,8},{8,12},{12,16},{16,20},{20,24},{24,28},{28,32},{32,36}... | collective-permute-start | bytes 1572872 | tf_op jit(solution)/shard_map/ppermute | solution.py:18
  71.0 13.6 %collective-permute-start.11 = (bf16[512,1,512]{0,2,1:T(8,128)(2,1)S(1)}, bf16[512,1,512]{0,2,1:T(8,128)(2,1)S(1)}, u32[]{:S(2)}, u32[]{:S(2)}) collective-permute-start(bf16[512,1,512]{0,2,1:T(8,128)(2,1)S(1)} %get-tuple-element.22), channel_id=1, source_target_pairs={{4,0},{8,4},{12,8},{16,12},{20,16},{24,20},{28,24},{32,28},{36,32}... | collective-permute-start | bytes 1572872 | tf_op jit(solution)/shard_map/ppermute | solution.py:19
  86.3 12.2 %copy-start.21 = (bf16[108,512]{1,0:T(8,128)(2,1)S(1)}, bf16[108,512]{1,0:T(8,128)(2,1)}, u32[]{:S(2)}) copy-start(bf16[108,512]{1,0:T(8,128)(2,1)} %copy-done.19) | copy-start | bytes 331780
  86.8 11.5 %copy-start.15 = (f32[1,12,2,512]{3,2,1,0:T(2,128)}, f32[1,12,2,512]{3,2,1,0:T(2,128)S(1)}, u32[]{:S(2)}) copy-start(f32[1,12,2,512]{3,2,1,0:T(2,128)S(1)} %get-tuple-element.14) | copy-start | bytes 147460
  86.9 9.1 %collective-permute-start.12 = (bf16[12,1,512]{2,1,0:T(2,128)(2,1)S(1)}, bf16[12,1,512]{2,1,0:T(2,128)(2,1)S(1)}, u32[]{:S(2)}, u32[]{:S(2)}) collective-permute-start(bf16[12,1,512]{2,1,0:T(2,128)(2,1)S(1)} %get-tuple-element.39), channel_id=1, source_target_pairs={{0,4},{4,8},{8,12},{12,16},{16,20},{20,24},{24,28},{28,32},{32,36}... | collective-permute-start | bytes 36872 | tf_op jit(solution)/shard_map/ppermute | solution.py:18
  88.8 8.6 %collective-permute-start.13 = (bf16[12,1,512]{2,1,0:T(2,128)(2,1)S(1)}, bf16[12,1,512]{2,1,0:T(2,128)(2,1)S(1)}, u32[]{:S(2)}, u32[]{:S(2)}) collective-permute-start(bf16[12,1,512]{2,1,0:T(2,128)(2,1)S(1)} %get-tuple-element.40), channel_id=1, source_target_pairs={{4,0},{8,4},{12,8},{16,12},{20,16},{24,20},{28,24},{32,28},{36,32}... | collective-permute-start | bytes 36872 | tf_op jit(solution)/shard_map/ppermute | solution.py:19
  102.8 10.0 %copy-start.8 = (bf16[3,3,12,512]{3,2,1,0:T(8,128)(2,1)S(1)}, bf16[3,3,12,512]{3,2,1,0:T(8,128)(2,1)}, u32[]{:S(2)}) copy-start(bf16[3,3,12,512]{3,2,1,0:T(8,128)(2,1)} %param.18) | copy-start | bytes 331780
  103.9 19.3 %collective-permute-start.14 = (bf16[512,1,512]{0,2,1:T(8,128)(2,1)}, bf16[512,1,512]{0,2,1:T(8,128)(2,1)}, u32[]{:S(2)}, u32[]{:S(2)}) collective-permute-start(bf16[512,1,512]{0,2,1:T(8,128)(2,1)} %get-tuple-element.19), channel_id=1, source_target_pairs={{0,4},{4,8},{8,12},{12,16},{16,20},{20,24},{24,28},{28,32},{32,36}... | collective-permute-start | bytes 1572872 | tf_op jit(solution)/shard_map/ppermute | solution.py:18
  105.8 17.4 %collective-permute-start.15 = (bf16[512,1,512]{0,2,1:T(8,128)(2,1)}, bf16[512,1,512]{0,2,1:T(8,128)(2,1)}, u32[]{:S(2)}, u32[]{:S(2)}) collective-permute-start(bf16[512,1,512]{0,2,1:T(8,128)(2,1)} %get-tuple-element.20), channel_id=1, source_target_pairs={{4,0},{8,4},{12,8},{16,12},{20,16},{24,20},{28,24},{32,28},{36,32}... | collective-permute-start | bytes 1572872 | tf_op jit(solution)/shard_map/ppermute | solution.py:19
  114.4 21.2 %collective-permute-start.2 = (bf16[512,1,512]{0,2,1:T(8,128)(2,1)}, bf16[512,1,512]{0,2,1:T(8,128)(2,1)}, u32[]{:S(2)}, u32[]{:S(2)}) collective-permute-start(bf16[512,1,512]{0,2,1:T(8,128)(2,1)} %get-tuple-element.25), channel_id=1, source_target_pairs={{0,4},{4,8},{8,12},{12,16},{16,20},{20,24},{24,28},{28,32},{32,36}... | collective-permute-start | bytes 1572872 | tf_op jit(solution)/shard_map/ppermute | solution.py:18
  116.3 19.3 %collective-permute-start.3 = (bf16[512,1,512]{0,2,1:T(8,128)(2,1)S(1)}, bf16[512,1,512]{0,2,1:T(8,128)(2,1)}, u32[]{:S(2)}, u32[]{:S(2)}) collective-permute-start(bf16[512,1,512]{0,2,1:T(8,128)(2,1)S(1)} %get-tuple-element.26), channel_id=1, source_target_pairs={{4,0},{8,4},{12,8},{16,12},{20,16},{24,20},{28,24},{32,28},{36,32}... | collective-permute-start | bytes 1572872 | tf_op jit(solution)/shard_map/ppermute | solution.py:19
  126.1 9.5 %copy-start.2 = (bf16[512,1024]{0,1:T(8,128)(2,1)S(1)}, bf16[512,1024]{0,1:T(8,128)(2,1)}, u32[]{:S(2)}) copy-start(bf16[512,1024]{0,1:T(8,128)(2,1)} %copy-done.1) | copy-start | bytes 3145732
  126.7 10.9 %copy-start.17 = (f32[1,12,2,512]{3,2,1,0:T(2,128)}, f32[1,12,2,512]{3,2,1,0:T(2,128)S(1)}, u32[]{:S(2)}) copy-start(f32[1,12,2,512]{3,2,1,0:T(2,128)S(1)} %get-tuple-element.12) | copy-start | bytes 147460
  126.7 10.4 %collective-permute-start.16 = (bf16[12,1,512]{2,1,0:T(2,128)(2,1)S(1)}, bf16[12,1,512]{2,1,0:T(2,128)(2,1)S(1)}, u32[]{:S(2)}, u32[]{:S(2)}) collective-permute-start(bf16[12,1,512]{2,1,0:T(2,128)(2,1)S(1)} %get-tuple-element.37), channel_id=1, source_target_pairs={{0,4},{4,8},{8,12},{12,16},{16,20},{20,24},{24,28},{28,32},{32,36}... | collective-permute-start | bytes 36872 | tf_op jit(solution)/shard_map/ppermute | solution.py:18
  128.6 8.5 %collective-permute-start.17 = (bf16[12,1,512]{2,1,0:T(2,128)(2,1)S(1)}, bf16[12,1,512]{2,1,0:T(2,128)(2,1)S(1)}, u32[]{:S(2)}, u32[]{:S(2)}) collective-permute-start(bf16[12,1,512]{2,1,0:T(2,128)(2,1)S(1)} %get-tuple-element.38), channel_id=1, source_target_pairs={{4,0},{8,4},{12,8},{16,12},{20,16},{24,20},{28,24},{32,28},{36,32}... | collective-permute-start | bytes 36872 | tf_op jit(solution)/shard_map/ppermute | solution.py:19
  143.5 11.4 %copy-start.9 = (bf16[108,512]{1,0:T(8,128)(2,1)S(1)}, bf16[108,512]{1,0:T(8,128)(2,1)}, u32[]{:S(2)}) copy-start(bf16[108,512]{1,0:T(8,128)(2,1)} %reshape.103) | copy-start | bytes 331780
  145.8 14.1 %collective-permute-start.18 = (bf16[512,1,512]{0,2,1:T(8,128)(2,1)}, bf16[512,1,512]{0,2,1:T(8,128)(2,1)}, u32[]{:S(2)}, u32[]{:S(2)}) collective-permute-start(bf16[512,1,512]{0,2,1:T(8,128)(2,1)} %get-tuple-element.17), channel_id=1, source_target_pairs={{0,4},{4,8},{8,12},{12,16},{16,20},{20,24},{24,28},{28,32},{32,36}... | collective-permute-start | bytes 1572872 | tf_op jit(solution)/shard_map/ppermute | solution.py:18
  147.7 14.0 %collective-permute-start.19 = (bf16[512,1,512]{0,2,1:T(8,128)(2,1)}, bf16[512,1,512]{0,2,1:T(8,128)(2,1)}, u32[]{:S(2)}, u32[]{:S(2)}) collective-permute-start(bf16[512,1,512]{0,2,1:T(8,128)(2,1)} %get-tuple-element.18), channel_id=1, source_target_pairs={{4,0},{8,4},{12,8},{16,12},{20,16},{24,20},{28,24},{32,28},{36,32}... | collective-permute-start | bytes 1572872 | tf_op jit(solution)/shard_map/ppermute | solution.py:19
  155.7 6.0 %copy-start.3 = (bf16[512,1024]{0,1:T(8,128)(2,1)S(1)}, bf16[512,1024]{0,1:T(8,128)(2,1)}, u32[]{:S(2)}) copy-start(bf16[512,1024]{0,1:T(8,128)(2,1)} %fusion) | copy-start | bytes 3145732
  156.8 6.4 %copy-start.5 = (bf16[108,512]{1,0:T(8,128)(2,1)S(1)}, bf16[108,512]{1,0:T(8,128)(2,1)}, u32[]{:S(2)}) copy-start(bf16[108,512]{1,0:T(8,128)(2,1)} %copy-done.4) | copy-start | bytes 331780
  163.9 1.1 copy-start.11
  163.9 1.1 copy-start.12
  163.9 1.1 copy-start.14
  (3 other events, 3.4 us)
where the time goes:
time: 423 us; the launch traced here: 422 us
  blocking collectives  253 us (60%)
  starting transfers between devices  89.7 us (21%)
  matrix products  25.5 us (6%)
  waiting for transfers between devices  21 us (5%)
  local copies, waits for them, and re-layouts  15.4 us (4%)
  other arithmetic  13.8 us (3%)
    psum x1, blocking collectives, per_device(): overall = lax.psum(jnp.sum(bits_map), 'rows')  253 us
    ppermute x10, starting transfers between devices, extended_2(): after = lax.ppermute(first, axis, down)  70.5 us
    ppermute x10, starting transfers between devices, extended_2(): before = lax.ppermute(last, axis, up)  19.2 us
    dot_general x4, matrix products, per_device(): back_in = jnp.dot(mid_weight, back_mid, preferred_element_type=jnp.float32)  18.7 us
    ppermute x10, waiting for transfers between devices, extended_2(): before = lax.ppermute(last, axis, up)  13.1 us
  transfers between devices with their start and end apart: 20, of which 8 were waited for; matrix products, arithmetic and copies ran while one was open for 3% of the time, Pallas kernels for 0%

commit v1 on v0

v1 whole, which is shorter than its diff:
```python
import functools
import math

import jax
import jax.numpy as jnp
from jax import lax
from jax.experimental import pallas as pl
from jax.experimental.pallas import tpu as pltpu
from jax.sharding import PartitionSpec as P

TERMS = 4
CH = 16
TAPS = 9 * CH
TILE = 256
MESH = pl.DeviceIdType.MESH


def from_left(x):
    lane = lax.broadcasted_iota(jnp.int32, x.shape, 1)
    return jnp.where(lane == 0, 0.0, pltpu.roll(x, 1, 1))


def from_right(x):
    last = x.shape[1] - 1
    lane = lax.broadcasted_iota(jnp.int32, x.shape, 1)
    return jnp.where(lane == last, 0.0, pltpu.roll(x, last, 1))


def fill_columns(columns, rows, flipped):
    width = rows[0].shape[1]
    for s, row in enumerate(rows):
        for j in range(3):
            if j == 1:
                piece = row
            elif (j == 0) != flipped:
                piece = from_left(row)
            else:
                piece = from_right(row)
            piece = piece.astype(jnp.bfloat16)
            for out_row in range(2):
                i = out_row + 2 - s if flipped else s - out_row
                if 0 <= i <= 2:
                    at = CH * (3 * i + j)
                    columns[at : at + CH, width * out_row : width * (out_row + 1)] = piece


def gather_taps(taps, width, flipped):
    def block(i, j, s):
        at = CH * (3 * i + j)
        return taps[at : at + CH, width * s : width * (s + 1)]

    result = []
    for d in range(4):
        total = None
        for j in range(3):
            part = None
            for s in range(2):
                i = d - s if flipped else s + 2 - d
                if 0 <= i <= 2:
                    value = block(i, j, s)
                    part = value if part is None else part + value
            if j != 1:
                part = from_right(part) if (j == 0) == flipped else from_left(part)
            total = part if total is None else total + part
        result.append(total)
    return result


def kernel(
    n_rows,
    group,
    pixels,
    probes,
    in_weight,
    in_bias,
    in_beta,
    mid_weight,
    mid_bias,
    mid_beta,
    out_weight,
    out_bias,
    latent_ref,
    bits_ref,
    mean_ref,
    pad_rows,
    weight_pad,
    in_plain,
    in_turned,
    out_plain,
    out_turned,
    mid_turned,
    columns,
    in_slope,
    mid_slope,
    act_a,
    act_b,
    act_c,
    taps,
    halo_send,
    halo_recv,
    lat_send,
    lat_recv,
    last_send,
    last_recv,
    mine,
    group_sums,
    ring_mine,
    ring_sums,
    send_sem,
    recv_sem,
    sum_send_sem,
    group_sem,
    ring_sem,
):
    channels, height, width = pixels.shape
    hidden = mid_weight.shape[0]
    me = lax.axis_index("rows")
    up = lax.rem(me + n_rows - 1, n_rows)
    down = lax.rem(me + 1, n_rows)
    ring = n_rows // group
    q = lax.rem(me, group)
    z = me // group
    group_peers = [z * group + lax.rem(q + d, group) for d in range(1, group)]
    ring_peers = [lax.rem(z + d, ring) * group + q for d in range(1, ring)]
    is_first = me == 0
    is_last = me == n_rows - 1

    barrier = pltpu.get_barrier_semaphore()
    peers = [up, down] + group_peers + ring_peers
    for peer in peers:
        pl.semaphore_signal(barrier, inc=1, device_id={"rows": peer}, device_id_type=MESH)

    pad_rows[...] = jnp.zeros_like(pad_rows)
    for r in range(height):
        pad_rows[r, 0:channels, :] = pixels[:, r, :]
        pad_rows[height + r, 0:channels, :] = (2 * probes[:, r, :] - 1).astype(jnp.float32)
    for side in range(2):
        halo_send[0, side, 0:CH, :] = pad_rows[side].astype(jnp.bfloat16)
        halo_send[0, side, CH : 2 * CH, :] = pad_rows[2 + side].astype(jnp.bfloat16)

    pl.semaphore_wait(barrier, len(peers))

    def exchange(send, recv, index):
        made = []
        for side, peer in enumerate((up, down)):
            copy = pltpu.make_async_remote_copy(
                src_ref=send.at[side],
                dst_ref=recv.at[1 - side],
                send_sem=send_sem.at[index, side],
                recv_sem=recv_sem.at[index, 1 - side],
                device_id={"rows": peer},
                device_id_type=MESH,
            )
            copy.start()
            made.append(copy)
        return made

    def finish(made):
        for copy in made:
            copy.wait()

    def inside(value, outside):
        return jnp.where(outside, 0.0, value)

    first = exchange(halo_send.at[0], halo_recv.at[0], 0)

    weight_pad[...] = jnp.zeros_like(weight_pad)
    for source, plain, turned in ((in_weight, in_plain, in_turned), (out_weight, out_plain, out_turned)):
        for i in range(3):
            for j in range(3):
                at = CH * (3 * i + j)
                weight_pad[at : at + channels, :] = source[i, j].astype(jnp.float32)
        whole = weight_pad[...]
        plain[...] = whole[:TAPS].astype(jnp.bfloat16)
        turned[...] = whole.T[:, :TAPS].astype(jnp.bfloat16)
    mid_turned[...] = mid_weight[...].T

    finish(first)
    top, bottom = (halo_recv[0, side].astype(jnp.float32) for side in range(2))
    pix_rows = [inside(top[:CH], is_first), pad_rows[0], pad_rows[1], inside(bottom[:CH], is_last)]
    signs = [inside(top[CH:], is_first), pad_rows[2], pad_rows[3], inside(bottom[CH:], is_last)]

    tiles = [slice(at, at + TILE) for at in range(0, height * width, TILE)]

    def dot(a, b):
        return jnp.dot(a, b, preferred_element_type=jnp.float32)

    scale = 0.5 / 1.1

    def lip(value, half_rate):
        half = half_rate * value
        t = jnp.tanh(half)
        gate = scale * (1.0 + t)
        return gate * value, gate * (1.0 + half * (1.0 - t))

    fill_columns(columns, pix_rows, False)
    in_b = in_bias[...]
    in_r = 0.5 * in_beta[...]
    mid_b = mid_bias[...]
    mid_r = 0.5 * mid_beta[...]
    for t in tiles:
        act, slope = lip(dot(in_turned[...], columns[:, t]) + in_b, in_r)
        act_a[:, t] = act.astype(jnp.bfloat16)
        in_slope[:, t] = slope
    for t in tiles:
        act, slope = lip(dot(mid_turned[...], act_a[:, t]) + mid_b, mid_r)
        act_c[:, t] = act.astype(jnp.bfloat16)
        mid_slope[:, t] = slope

    def pull_back(rows):
        fill_columns(columns, rows, True)
        for t in tiles:
            act_a[:, t] = (dot(out_turned[...], columns[:, t]) * mid_slope[:, t]).astype(jnp.bfloat16)
        for t in tiles:
            act_b[:, t] = (dot(mid_weight[...], act_a[:, t]) * in_slope[:, t]).astype(jnp.bfloat16)
        for t in tiles:
            taps[:, t] = dot(in_plain[...], act_b[:, t])
        return gather_taps(taps, width, True)

    vector = signs
    logdet = [jnp.zeros((1, width), jnp.float32) for _ in range(height)]
    log_prior = None
    latent_out = None
    for term in range(1, TERMS):
        parts = pull_back(vector)
        for side in range(2):
            for r in range(2):
                halo_send[term, side, CH * r : CH * (r + 1), :] = parts[2 * side + r].astype(jnp.bfloat16)
        moving = exchange(halo_send.at[term], halo_recv.at[term], term)
        if term == 1:
            for t in tiles:
                taps[:, t] = dot(out_plain[...], act_c[:, t])
            branch = gather_taps(taps, width, False)
            lat_send[0] = branch[0].astype(jnp.bfloat16)
            lat_send[1] = branch[3].astype(jnp.bfloat16)
            lat_moving = exchange(lat_send, lat_recv, TERMS)
        if term == 2:
            finish(lat_moving)
            outer = [inside(lat_recv[side].astype(jnp.float32), where) for side, where in enumerate((is_first, is_last))]
            log_prior = []
            for r in range(height):
                whole = branch[1 + r] + outer[r]
                latent = pixels[:, r, :] + (whole[:channels] + out_bias[...])
                latent_ref[:, r, :] = latent
                log_prior.append(-0.5 * jnp.sum(latent * latent, axis=0, keepdims=True))
        finish(moving)
        top = inside(halo_recv[term, 0].astype(jnp.float32), is_first)
        bottom = inside(halo_recv[term, 1].astype(jnp.float32), is_last)
        vector = [
            inside(parts[0], is_first) + top[:CH],
            parts[1] + top[CH:],
            parts[2] + bottom[:CH],
            inside(parts[3], is_last) + bottom[CH:],
        ]
        weight = (-1.0) ** (term + 1) / term
        for r in range(height):
            logdet[r] = logdet[r] + weight * jnp.sum(vector[1 + r] * signs[1 + r], axis=0, keepdims=True)

    parts = pull_back(vector)
    weight = (-1.0) ** (TERMS + 1) / TERMS
    dots = [weight * jnp.sum(part * sign, axis=0, keepdims=True) for part, sign in zip(parts, signs)]
    last_send[0] = dots[0]
    last_send[1] = dots[3]
    moving = exchange(last_send, last_recv, TERMS + 1)
    known = [log_prior[r] + logdet[r] + dots[1 + r] for r in range(height)]
    total = (known[0] + known[1]) + (dots[0] + dots[3])
    lanes = total[:, 0:128]
    for at in range(128, width, 128):
        lanes = lanes + total[:, at : at + 128]

    def spread(value, own, slots, slot, others, sems, send_at):
        own[...] = value
        made = []
        for d, peer in enumerate(others):
            copy = pltpu.make_async_remote_copy(
                src_ref=own,
                dst_ref=slots.at[slot],
                send_sem=sum_send_sem.at[send_at + d],
                recv_sem=sems.at[slot],
                device_id={"rows": peer},
                device_id_type=MESH,
            )
            copy.start()
            made.append(copy)
        slots[slot] = value
        return made

    def collect(own, slots, slot, sems, count):
        for d in range(1, count):
            other = lax.rem(slot + d, count)
            pltpu.make_async_copy(own, slots.at[other], sems.at[other]).wait()
        value = slots[0]
        for d in range(1, count):
            value = value + slots[d]
        return value

    sums = spread(lanes, mine, group_sums, q, group_peers, group_sem, 0)
    lanes = collect(mine, group_sums, q, group_sem, group)
    sums += spread(lanes, ring_mine, ring_sums, z, ring_peers, ring_sem, group - 1)

    finish(moving)
    spare = [inside(last_recv[side], where) for side, where in enumerate((is_first, is_last))]
    base = 8.0 + 0.5 * math.log(2.0 * math.pi) / math.log(2.0)
    rate = 1.0 / (channels * math.log(2.0))
    for r in range(height):
        bits_ref[r : r + 1, :] = base - rate * (known[r] + spare[r])

    lanes = collect(ring_mine, ring_sums, z, ring_sem, ring)
    mean_ref[0] = base - jnp.sum(lanes) * (rate / (n_rows * height * width))
    for copy in sums:
        copy.wait_send()


def solution(mesh):
    n_rows = mesh.shape["rows"]
    group = min(8, n_rows // 2)
    ring = n_rows // group

    def per_device(
        pixels, probes, in_weight, in_bias, in_beta, mid_weight, mid_bias, mid_beta, out_weight, out_bias
    ):
        channels, height, width = pixels.shape
        hidden = mid_weight.shape[0]
        area = height * width
        f32, bf16 = jnp.float32, jnp.bfloat16
        vmem = pl.BlockSpec(memory_space=pltpu.VMEM)
        return pl.pallas_call(
            functools.partial(kernel, n_rows, group),
            out_shape=(
                jax.ShapeDtypeStruct((channels, height, width), f32),
                jax.ShapeDtypeStruct((height, width), f32),
                jax.ShapeDtypeStruct((1,), f32),
            ),
            in_specs=[vmem] * 10,
            out_specs=(vmem, vmem, pl.BlockSpec(memory_space=pltpu.SMEM)),
            scratch_shapes=[
                pltpu.VMEM((4, CH, width), f32),
                pltpu.VMEM((256, hidden), f32),
                pltpu.VMEM((TAPS, hidden), bf16),
                pltpu.VMEM((hidden, TAPS), bf16),
                pltpu.VMEM((TAPS, hidden), bf16),
                pltpu.VMEM((hidden, TAPS), bf16),
                pltpu.VMEM((hidden, hidden), bf16),
                pltpu.VMEM((TAPS, area), bf16),
                pltpu.VMEM((hidden, area), f32),
                pltpu.VMEM((hidden, area), f32),
                pltpu.VMEM((hidden, area), bf16),
                pltpu.VMEM((hidden, area), bf16),
                pltpu.VMEM((hidden, area), bf16),
                pltpu.VMEM((TAPS, area), f32),
                pltpu.VMEM((TERMS, 2, 2 * CH, width), bf16),
                pltpu.VMEM((TERMS, 2, 2 * CH, width), bf16),
                pltpu.VMEM((2, CH, width), bf16),
                pltpu.VMEM((2, CH, width), bf16),
                pltpu.VMEM((2, 1, width), f32),
                pltpu.VMEM((2, 1, width), f32),
                pltpu.VMEM((1, 128), f32),
                pltpu.VMEM((group, 1, 128), f32),
                pltpu.VMEM((1, 128), f32),
                pltpu.VMEM((ring, 1, 128), f32),
                pltpu.SemaphoreType.DMA((TERMS + 2, 2)),
                pltpu.SemaphoreType.DMA((TERMS + 2, 2)),
                pltpu.SemaphoreType.DMA((group + ring - 2,)),
                pltpu.SemaphoreType.DMA((group,)),
                pltpu.SemaphoreType.DMA((ring,)),
            ],
            compiler_params=pltpu.CompilerParams(
                collective_id=0, has_side_effects=True, vmem_limit_bytes=40 * 1024 * 1024
            ),
        )(
            pixels,
            probes,
            in_weight,
            in_bias[:, None],
            in_beta[:, None],
            mid_weight,
            mid_bias[:, None],
            mid_beta[:, None],
            out_weight,
            out_bias[:, None],
        )

    placed = (P("batch", "rows", None),) * 2 + (P(),) * 8
    return jax.shard_map(
        per_device,
        mesh=mesh,
        in_specs=placed,
        out_specs=(P("batch", "rows", None), P(("batch", "rows"), None), P("batch")),
        check_vma=False,
    )
```

time: 423 us -> 55.6 us (0.13)
  the two profiles are of different devices: /device:TPU:392 before, /device:TPU:1 now
where the time goes in v1:
time: 55.6 us; the launch traced here: 55.3 us
  Pallas kernels  47.9 us (86%)
  local copies, waits for them, and re-layouts  4.94 us (9%)
  between operations  2.47 us (4%)
    pallas_call x1, Pallas kernels, per_device(): pl.pallas_call(functools.partial(kernel, n_rows, group), out_shape=(jax.S...  47.9 us
    unnamed x22, local copies, waits for them, and re-layouts  4.27 us

profile of v1, /device:TPU:1, one launch (start us, length us, event | category | flops | bytes accessed | tf_op | source)
XLA Modules:
  0.0 55.3 jit_solution(11670779792728979921)
XLA Ops:
  0.6 0.0 copy-start.9
  0.6 0.6 %copy-done.9 = f32[12]{0:T(128)S(1)} copy-done((f32[12]{0:T(128)S(1)}, f32[12]{0:T(128)}, u32[]{:S(2)}) %copy-start.9) | copy-done | bytes 72
  1.3 0.0 copy-start.5
  1.3 0.0 copy-start.6
  1.3 0.1 copy.18.out_bias
  1.4 0.6 %copy-done.5 = f32[512]{0:T(512)S(1)} copy-done((f32[512]{0:T(512)S(1)}, f32[512]{0:T(512)}, u32[]{:S(2)}) %copy-start.5) | copy-done | bytes 2072
  2.0 0.0 copy-start
  2.0 0.1 copy.14.in_bias
  2.1 0.0 copy-done.6
  2.1 0.0 copy-start.7
  2.1 0.1 copy.15.in_beta
  2.3 0.5 copy-done.7
  2.8 0.0 copy-start.8
  2.8 0.0 copy-start.2
  2.8 0.1 copy.16.mid_bias
  3.0 0.5 copy-done.8
  3.5 0.0 copy-start.1
  3.5 0.0 copy-start.3
  3.5 0.0 copy-start.4
  3.5 0.1 copy.17.mid_beta
  3.7 0.0 copy-done
  3.7 0.1 copy-done.2
  3.8 0.6 %copy-done.1 = bf16[3,3,12,512]{3,2,1,0:T(8,128)(2,1)S(1)} copy-done((bf16[3,3,12,512]{3,2,1,0:T(8,128)(2,1)S(1)}, bf16[3,3,12,512]{3,2,1,0:T(8,128)(2,1)}, u32[]{:S(2)}) %copy-start.1) | copy-done | bytes 110616
  4.4 0.0 copy-done.3
  4.4 0.0 copy-done.4
  4.4 47.9 %shard_map.121 = (f32[12,2,512]{2,1,0:T(2,128)S(1)}, f32[2,512]{1,0:T(2,128)S(1)}, f32[1]{0:T(128)}) custom-call(f32[12,2,512]{2,1,0:T(2,128)S(1)} %copy-done.3, s32[12,2,512]{2,1,0:T(2,128)S(1)} %copy-done.4, bf16[3,3,12,512]{3,2,1,0:T(8,128)(2,1)S(1)} %copy-done.1, f32[512,1]{1,0:T(8,128)S(1)} %copy.14.in_bias, f32[512,1]{1,0:T(8,128)S(1)} %copy.15.in_beta, ...), custom_call_target="tpu_custom_call" | custom-call | tf_op jit(solution)/shard_map/pallas_call | solution.py:327
  52.3 0.6 %copy.22 = f32[12,2,512]{2,1,0:T(2,128)} copy(f32[12,2,512]{2,1,0:T(2,128)S(1)} %get-tuple-element.6) | data formatting | bytes 98304
  52.9 0.6 %copy.23 = f32[2,512]{1,0:T(2,128)} copy(f32[2,512]{1,0:T(2,128)S(1)} %get-tuple-element.7) | data formatting | bytes 8192
Async XLA Ops:
  0.6 0.7 %copy-start.9 = (f32[12]{0:T(128)S(1)}, f32[12]{0:T(128)}, u32[]{:S(2)}) copy-start(f32[12]{0:T(128)} %param.19) | copy-start | bytes 148
  1.3 0.7 %copy-start.5 = (f32[512]{0:T(512)S(1)}, f32[512]{0:T(512)}, u32[]{:S(2)}) copy-start(f32[512]{0:T(512)} %param.13) | copy-start | bytes 6148
  1.3 0.8 %copy-start.6 = (f32[512]{0:T(512)S(1)}, f32[512]{0:T(512)}, u32[]{:S(2)}) copy-start(f32[512]{0:T(512)} %param.14) | copy-start | bytes 6148
  2.0 1.7 %copy-start = (bf16[512,512]{1,0:T(8,128)(2,1)S(1)}, bf16[512,512]{1,0:T(8,128)(2,1)}, u32[]{:S(2)}) copy-start(bf16[512,512]{1,0:T(8,128)(2,1)} %mid_weight.1) | copy-start | bytes 1572868
  2.1 0.7 %copy-start.7 = (f32[512]{0:T(512)S(1)}, f32[512]{0:T(512)}, u32[]{:S(2)}) copy-start(f32[512]{0:T(512)} %param.16) | copy-start | bytes 6148
  2.8 0.7 %copy-start.8 = (f32[512]{0:T(512)S(1)}, f32[512]{0:T(512)}, u32[]{:S(2)}) copy-start(f32[512]{0:T(512)} %param.17) | copy-start | bytes 6148
  2.8 1.0 %copy-start.2 = (bf16[3,3,12,512]{3,2,1,0:T(8,128)(2,1)S(1)}, bf16[3,3,12,512]{3,2,1,0:T(8,128)(2,1)}, u32[]{:S(2)}) copy-start(bf16[3,3,12,512]{3,2,1,0:T(8,128)(2,1)} %out_weight.1) | copy-start | bytes 331780
  3.5 0.9 %copy-start.1 = (bf16[3,3,12,512]{3,2,1,0:T(8,128)(2,1)S(1)}, bf16[3,3,12,512]{3,2,1,0:T(8,128)(2,1)}, u32[]{:S(2)}) copy-start(bf16[3,3,12,512]{3,2,1,0:T(8,128)(2,1)} %in_weight.1) | copy-start | bytes 331780
  3.5 0.9 %copy-start.3 = (f32[12,2,512]{2,1,0:T(2,128)S(1)}, f32[12,2,512]{2,1,0:T(2,128)}, u32[]{:S(2)}) copy-start(f32[12,2,512]{2,1,0:T(2,128)} %pixels.1) | copy-start | bytes 147460
  3.5 0.9 %copy-start.4 = (s32[12,2,512]{2,1,0:T(2,128)S(1)}, s32[12,2,512]{2,1,0:T(2,128)}, u32[]{:S(2)}) copy-start(s32[12,2,512]{2,1,0:T(2,128)} %probes.1) | copy-start | bytes 147460

commit v2 on v1

--- a/solution.py
+++ b/solution.py
@@ -69,6 +69,19 @@
 def kernel(
     n_rows,
     group,
+    pixels_hbm,
+    probes_hbm,
+    in_weight_hbm,
+    in_bias_hbm,
+    in_beta_hbm,
+    mid_weight_hbm,
+    mid_bias_hbm,
+    mid_beta_hbm,
+    out_weight_hbm,
+    out_bias_hbm,
+    latent_ref,
+    bits_ref,
+    mean_ref,
     pixels,
     probes,
     in_weight,
@@ -79,10 +92,9 @@
     mid_beta,
     out_weight,
     out_bias,
-    latent_ref,
-    bits_ref,
-    mean_ref,
+    load_sem,
     pad_rows,
+    small_pad,
     weight_pad,
     in_plain,
     in_turned,
@@ -98,6 +110,8 @@
     taps,
     halo_send,
     halo_recv,
+    pair_send,
+    pair_recv,
     lat_send,
     lat_recv,
     last_send,
@@ -111,9 +125,9 @@
     sum_send_sem,
     group_sem,
     ring_sem,
+    known_sem,
 ):
     channels, height, width = pixels.shape
-    hidden = mid_weight.shape[0]
     me = lax.axis_index("rows")
     up = lax.rem(me + n_rows - 1, n_rows)
     down = lax.rem(me + 1, n_rows)
@@ -125,11 +139,53 @@
     is_first = me == 0
     is_last = me == n_rows - 1
 
+    sources = (
+        pixels_hbm,
+        probes_hbm,
+        in_bias_hbm,
+        in_beta_hbm,
+        mid_bias_hbm,
+        mid_beta_hbm,
+        out_bias_hbm,
+        in_weight_hbm,
+        out_weight_hbm,
+        mid_weight_hbm,
+    )
+    places = (pixels, probes, in_bias, in_beta, mid_bias, mid_beta, out_bias, in_weight, out_weight, mid_weight)
+    loads = [
+        pltpu.make_async_copy(source, place, load_sem.at[k]) for k, (source, place) in enumerate(zip(sources, places))
+    ]
+    for load in loads[:2]:
+        load.start()
+
+    def signal(sem, peer):
+        pl.semaphore_signal(sem, inc=1, device_id={"rows": peer}, device_id_type=MESH)
+
+    def around(step):
+        return [lax.rem(z + d, ring) * group + q for d in (step, ring - step)]
+
     barrier = pltpu.get_barrier_semaphore()
-    peers = [up, down] + group_peers + ring_peers
-    for peer in peers:
-        pl.semaphore_signal(barrier, inc=1, device_id={"rows": peer}, device_id_type=MESH)
-
+    greeted = [up, down] + group_peers + around(1)
+    for peer in greeted:
+        signal(barrier, peer)
+    for load in loads[2:]:
+        load.start()
+
+    steps = []
+    while 2 ** len(steps) < ring // 2:
+        steps.append(2 ** len(steps))
+
+    def spread_word(k):
+        if k < len(steps):
+            for peer in around(steps[k]):
+                signal(known_sem.at[k], peer)
+
+    def hear_word(k):
+        if k < len(steps):
+            pl.semaphore_wait(known_sem.at[k], 2)
+
+    loads[0].wait()
+    loads[1].wait()
     pad_rows[...] = jnp.zeros_like(pad_rows)
     for r in range(height):
         pad_rows[r, 0:channels, :] = pixels[:, r, :]
@@ -138,7 +194,7 @@
         halo_send[0, side, 0:CH, :] = pad_rows[side].astype(jnp.bfloat16)
         halo_send[0, side, CH : 2 * CH, :] = pad_rows[2 + side].astype(jnp.bfloat16)
 
-    pl.semaphore_wait(barrier, len(peers))
+    pl.semaphore_wait(barrier, len(greeted))
 
     def exchange(send, recv, index):
         made = []
@@ -163,6 +219,19 @@
         return jnp.where(outside, 0.0, value)
 
     first = exchange(halo_send.at[0], halo_recv.at[0], 0)
+    spread_word(0)
+
+    for load in loads[2:]:
+        load.wait()
+    small_pad[...] = jnp.zeros_like(small_pad)
+    for k, vector_ref in enumerate((in_bias, in_beta, mid_bias, mid_beta)):
+        small_pad[k : k + 1, :] = vector_ref[...]
+    small_pad[4:5, 0:channels] = out_bias[...]
+    small = small_pad[...].T
+    in_b, in_r, mid_b, mid_r = (small[:, k : k + 1] for k in range(4))
+    in_r = 0.5 * in_r
+    mid_r = 0.5 * mid_r
+    out_b = small[:channels, 4:5]
 
     weight_pad[...] = jnp.zeros_like(weight_pad)
     for source, plain, turned in ((in_weight, in_plain, in_turned), (out_weight, out_plain, out_turned)):
@@ -194,10 +263,6 @@
         return gate * value, gate * (1.0 + half * (1.0 - t))
 
     fill_columns(columns, pix_rows, False)
-    in_b = in_bias[...]
-    in_r = 0.5 * in_beta[...]
-    mid_b = mid_bias[...]
-    mid_r = 0.5 * mid_beta[...]
     for t in tiles:
         act, slope = lip(dot(in_turned[...], columns[:, t]) + in_b, in_r)
         act_a[:, t] = act.astype(jnp.bfloat16)
@@ -217,53 +282,82 @@
             taps[:, t] = dot(in_plain[...], act_b[:, t])
         return gather_taps(taps, width, True)
 
-    vector = signs
-    logdet = [jnp.zeros((1, width), jnp.float32) for _ in range(height)]
-    log_prior = None
-    latent_out = None
-    for term in range(1, TERMS):
-        parts = pull_back(vector)
+    def push(rows):
+        fill_columns(columns, rows, False)
+        for t in tiles:
+            act_a[:, t] = (dot(in_turned[...], columns[:, t]) * in_slope[:, t]).astype(jnp.bfloat16)
+        for t in tiles:
+            act_b[:, t] = (dot(mid_turned[...], act_a[:, t]) * mid_slope[:, t]).astype(jnp.bfloat16)
+        for t in tiles:
+            taps[:, t] = dot(out_plain[...], act_b[:, t])
+        return gather_taps(taps, width, False)
+
+    def send_parts(parts, send, recv, index):
         for side in range(2):
             for r in range(2):
-                halo_send[term, side, CH * r : CH * (r + 1), :] = parts[2 * side + r].astype(jnp.bfloat16)
-        moving = exchange(halo_send.at[term], halo_recv.at[term], term)
-        if term == 1:
-            for t in tiles:
-                taps[:, t] = dot(out_plain[...], act_c[:, t])
-            branch = gather_taps(taps, width, False)
-            lat_send[0] = branch[0].astype(jnp.bfloat16)
-            lat_send[1] = branch[3].astype(jnp.bfloat16)
-            lat_moving = exchange(lat_send, lat_recv, TERMS)
-        if term == 2:
-            finish(lat_moving)
-            outer = [inside(lat_recv[side].astype(jnp.float32), where) for side, where in enumerate((is_first, is_last))]
-            log_prior = []
-            for r in range(height):
-                whole = branch[1 + r] + outer[r]
-                latent = pixels[:, r, :] + (whole[:channels] + out_bias[...])
-                latent_ref[:, r, :] = latent
-                log_prior.append(-0.5 * jnp.sum(latent * latent, axis=0, keepdims=True))
+                send[side, CH * r : CH * (r + 1), :] = parts[2 * side + r].astype(jnp.bfloat16)
+        return exchange(send, recv, index)
+
+    def whole_rows(parts, recv, moving):
         finish(moving)
-        top = inside(halo_recv[term, 0].astype(jnp.float32), is_first)
-        bottom = inside(halo_recv[term, 1].astype(jnp.float32), is_last)
-        vector = [
+        top = inside(recv[0].astype(jnp.float32), is_first)
+        bottom = inside(recv[1].astype(jnp.float32), is_last)
+        return [
             inside(parts[0], is_first) + top[:CH],
             parts[1] + top[CH:],
             parts[2] + bottom[:CH],
             inside(parts[3], is_last) + bottom[CH:],
         ]
-        weight = (-1.0) ** (term + 1) / term
-        for r in range(height):
-            logdet[r] = logdet[r] + weight * jnp.sum(vector[1 + r] * signs[1 + r], axis=0, keepdims=True)
+
+    def coefficient(term):
+        return (-1.0) ** (term + 1) / term
+
+    def add_term(logdet, rows, term):
+        return [
+            logdet[r] + coefficient(term) * jnp.sum(rows[1 + r] * signs[1 + r], axis=0, keepdims=True)
+            for r in range(height)
+        ]
+
+    logdet = [jnp.zeros((1, width), jnp.float32) for _ in range(height)]
+
+    parts = pull_back(signs)
+    moving = send_parts(parts, halo_send.at[1], halo_recv.at[1], 1)
+    hear_word(0)
+    spread_word(1)
+    for t in tiles:
+        taps[:, t] = dot(out_plain[...], act_c[:, t])
+    branch = gather_taps(taps, width, False)
+    lat_send[0] = branch[0].astype(jnp.bfloat16)
+    lat_send[1] = branch[3].astype(jnp.bfloat16)
+    lat_moving = exchange(lat_send, lat_recv, TERMS)
+    pushed_1 = push(signs)
+    pair_moving = send_parts(pushed_1, pair_send, pair_recv, TERMS + 2)
+    hear_word(1)
+    spread_word(2)
+    vector = whole_rows(parts, halo_recv.at[1], moving)
 
     parts = pull_back(vector)
-    weight = (-1.0) ** (TERMS + 1) / TERMS
-    dots = [weight * jnp.sum(part * sign, axis=0, keepdims=True) for part, sign in zip(parts, signs)]
-    last_send[0] = dots[0]
-    last_send[1] = dots[3]
-    moving = exchange(last_send, last_recv, TERMS + 1)
-    known = [log_prior[r] + logdet[r] + dots[1 + r] for r in range(height)]
-    total = (known[0] + known[1]) + (dots[0] + dots[3])
+    moving = send_parts(parts, halo_send.at[2], halo_recv.at[2], 2)
+    logdet = add_term(logdet, vector, 1)
+    finish(lat_moving)
+    outer = [inside(lat_recv[side].astype(jnp.float32), where) for side, where in enumerate((is_first, is_last))]
+    log_prior = []
+    for r in range(height):
+        whole = branch[1 + r] + outer[r]
+        latent = pixels[:, r, :] + (whole[:channels] + out_b)
+        latent_ref[:, r, :] = latent
+        log_prior.append(-0.5 * jnp.sum(latent * latent, axis=0, keepdims=True))
+    pushed_2 = push(whole_rows(pushed_1, pair_recv, pair_moving))
+    hear_word(2)
+    vector = whole_rows(parts, halo_recv.at[2], moving)
+
+    logdet = add_term(logdet, vector, 2)
+    total = (log_prior[0] + logdet[0]) + (log_prior[1] + logdet[1])
+    later = None
+    for d in range(4):
+        both = (coefficient(3) * pushed_1[d] + coefficient(4) * pushed_2[d]) * vector[d]
+        later = both if later is None else later + both
+    total = total + jnp.sum(later, axis=0, keepdims=True)
     lanes = total[:, 0:128]
     for at in range(128, width, 128):
         lanes = lanes + total[:, at : at + 128]
@@ -295,9 +389,20 @@
         return value
 
     sums = spread(lanes, mine, group_sums, q, group_peers, group_sem, 0)
+
+    parts = pull_back(vector)
+    moving = send_parts(parts, halo_send.at[3], halo_recv.at[3], 3)
     lanes = collect(mine, group_sums, q, group_sem, group)
     sums += spread(lanes, ring_mine, ring_sums, z, ring_peers, ring_sem, group - 1)
-
+    vector = whole_rows(parts, halo_recv.at[3], moving)
+
+    parts = pull_back(vector)
+    dots = [coefficient(4) * jnp.sum(part * sign, axis=0, keepdims=True) for part, sign in zip(parts, signs)]
+    last_send[0] = dots[0]
+    last_send[1] = dots[3]
+    moving = exchange(last_send, last_recv, TERMS + 1)
+    logdet = add_term(logdet, vector, 3)
+    known = [log_prior[r] + logdet[r] + dots[1 + r] for r in range(height)]
     finish(moving)
     spare = [inside(last_recv[side], where) for side, where in enumerate((is_first, is_last))]
     base = 8.0 + 0.5 * math.log(2.0 * math.pi) / math.log(2.0)
@@ -331,10 +436,22 @@
                 jax.ShapeDtypeStruct((height, width), f32),
                 jax.ShapeDtypeStruct((1,), f32),
             ),
-            in_specs=[vmem] * 10,
+            in_specs=[pl.BlockSpec(memory_space=pltpu.HBM)] * 10,
             out_specs=(vmem, vmem, pl.BlockSpec(memory_space=pltpu.SMEM)),
             scratch_shapes=[
+                pltpu.VMEM((channels, height, width), f32),
+                pltpu.VMEM((channels, height, width), probes.dtype),
+                pltpu.VMEM(in_weight.shape, bf16),
+                pltpu.VMEM((1, hidden), f32),
+                pltpu.VMEM((1, hidden), f32),
+                pltpu.VMEM((hidden, hidden), bf16),
+                pltpu.VMEM((1, hidden), f32),
+                pltpu.VMEM((1, hidden), f32),
+                pltpu.VMEM(out_weight.shape, bf16),
+                pltpu.VMEM((1, channels), f32),
+                pltpu.SemaphoreType.DMA((10,)),
                 pltpu.VMEM((4, CH, width), f32),
+                pltpu.VMEM((128, hidden), f32),
                 pltpu.VMEM((256, hidden), f32),
                 pltpu.VMEM((TAPS, hidden), bf16),
                 pltpu.VMEM((hidden, TAPS), bf16),
@@ -350,6 +467,8 @@
                 pltpu.VMEM((TAPS, area), f32),
                 pltpu.VMEM((TERMS, 2, 2 * CH, width), bf16),
                 pltpu.VMEM((TERMS, 2, 2 * CH, width), bf16),
+                pltpu.VMEM((2, 2 * CH, width), bf16),
+                pltpu.VMEM((2, 2 * CH, width), bf16),
                 pltpu.VMEM((2, CH, width), bf16),
                 pltpu.VMEM((2, CH, width), bf16),
                 pltpu.VMEM((2, 1, width), f32),
@@ -358,26 +477,27 @@
                 pltpu.VMEM((group, 1, 128), f32),
                 pltpu.VMEM((1, 128), f32),
                 pltpu.VMEM((ring, 1, 128), f32),
-                pltpu.SemaphoreType.DMA((TERMS + 2, 2)),
-                pltpu.SemaphoreType.DMA((TERMS + 2, 2)),
+                pltpu.SemaphoreType.DMA((TERMS + 3, 2)),
+                pltpu.SemaphoreType.DMA((TERMS + 3, 2)),
                 pltpu.SemaphoreType.DMA((group + ring - 2,)),
                 pltpu.SemaphoreType.DMA((group,)),
                 pltpu.SemaphoreType.DMA((ring,)),
+                pltpu.SemaphoreType.REGULAR((3,)),
             ],
             compiler_params=pltpu.CompilerParams(
-                collective_id=0, has_side_effects=True, vmem_limit_bytes=40 * 1024 * 1024
+                collective_id=0, has_side_effects=True, vmem_limit_bytes=60 * 1024 * 1024
             ),
         )(
             pixels,
             probes,
             in_weight,
-            in_bias[:, None],
-            in_beta[:, None],
+            in_bias[None, :],
+            in_beta[None, :],
             mid_weight,
-            mid_bias[:, None],
-            mid_beta[:, None],
+            mid_bias[None, :],
+            mid_beta[None, :],
             out_weight,
-            out_bias[:, None],
+            out_bias[None, :],
         )
 
     placed = (P("batch", "rows", None),) * 2 + (P(),) * 8

time: 55.6 us -> 45 us (0.81)
  the two profiles are of different devices: /device:TPU:1 before, /device:TPU:8 now
where the time goes in v2:
time: 45 us; the launch traced here: 44.8 us
  Pallas kernels  40.4 us (90%)
  between operations  2.34 us (5%)
  local copies, waits for them, and re-layouts  2.02 us (4%)
    pallas_call x1, Pallas kernels, per_device(): pl.pallas_call(functools.partial(kernel, n_rows, group), out_shape=(jax.S...  40.4 us
    unnamed x4, local copies, waits for them, and re-layouts  2.02 us

profile of v2, /device:TPU:8, one launch (start us, length us, event | category | flops | bytes accessed | tf_op | source)
XLA Modules:
  0.0 44.8 jit_solution(2007319161866230048)
XLA Ops:
  0.6 40.4 %shard_map.121 = (f32[12,2,512]{2,1,0:T(2,128)}, f32[2,512]{1,0:T(2,128)}, f32[1]{0:T(128)}) custom-call(f32[12,2,512]{2,1,0:T(2,128)} %pixels_hbm.1, s32[12,2,512]{2,1,0:T(2,128)} %probes_hbm.1, bf16[3,3,12,512]{3,2,1,0:T(8,128)(2,1)} %in_weight_hbm.1, f32[1,512]{1,0:T(1,128)} %bitcast.5, f32[1,512]{1,0:T(1,128)} %bitcast.6, ...), custom_call_target="tpu_custom_call" | custom-call | tf_op jit(solution)/shard_map/pallas_call | solution.py:432
  41.1 0.0 copy-start
  41.1 1.4 %copy.16 = f32[12,2,512]{2,1,0:T(2,128)} copy(f32[12,2,512]{2,1,0:T(2,128)} %get-tuple-element.6) | data formatting | bytes 98304
  42.5 0.0 copy-done
  42.5 0.6 %copy.17 = f32[2,512]{1,0:T(2,128)} copy(f32[2,512]{1,0:T(2,128)S(1)} %copy-done) | data formatting | bytes 8192
Async XLA Ops:
  41.1 1.4 %copy-start = (f32[2,512]{1,0:T(2,128)S(1)}, f32[2,512]{1,0:T(2,128)}, u32[]{:S(2)}) copy-start(f32[2,512]{1,0:T(2,128)} %get-tuple-element.7) | copy-start | bytes 12292

commit v3 on v2

--- a/solution.py
+++ b/solution.py
@@ -108,20 +108,30 @@
     act_b,
     act_c,
     taps,
+    slab_send,
+    slab_own,
+    slab_above,
+    slab_below,
     halo_send,
     halo_recv,
     pair_send,
     pair_recv,
     lat_send,
     lat_recv,
+    lat_own_send,
+    lat_own,
     last_send,
     last_recv,
+    last_own_send,
+    last_own,
     mine,
     group_sums,
     ring_mine,
     ring_sums,
     send_sem,
     recv_sem,
+    three_send,
+    three_recv,
     sum_send_sem,
     group_sem,
     ring_sem,
@@ -129,15 +139,29 @@
 ):
     channels, height, width = pixels.shape
     me = lax.axis_index("rows")
-    up = lax.rem(me + n_rows - 1, n_rows)
-    down = lax.rem(me + 1, n_rows)
     ring = n_rows // group
     q = lax.rem(me, group)
     z = me // group
     group_peers = [z * group + lax.rem(q + d, group) for d in range(1, group)]
     ring_peers = [lax.rem(z + d, ring) * group + q for d in range(1, ring)]
-    is_first = me == 0
-    is_last = me == n_rows - 1
+
+    def worker(slab):
+        layer = slab // group
+        s = lax.rem(slab, group)
+        back = group - 1 - s
+        swapped = back + 1 - 2 * lax.rem(back, 2)
+        return layer * group + s + lax.rem(layer, 2) * (swapped - s)
+
+    def step(slab, by):
+        return lax.rem(slab + n_rows + by, n_rows)
+
+    slab = worker(me)
+    stays = slab == me
+    owners = (step(slab, -1), slab, step(slab, 1))
+    workers = (worker(step(me, -1)), slab, worker(step(me, 1)))
+    up, down = worker(owners[0]), worker(owners[2])
+    edges_slab = (slab == 0, slab == n_rows - 1)
+    edges_own = (me == 0, me == n_rows - 1)
 
     sources = (
         pixels_hbm,
@@ -161,11 +185,11 @@
     def signal(sem, peer):
         pl.semaphore_signal(sem, inc=1, device_id={"rows": peer}, device_id_type=MESH)
 
-    def around(step):
-        return [lax.rem(z + d, ring) * group + q for d in (step, ring - step)]
+    def around(by):
+        return [lax.rem(z + d, ring) * group + q for d in (by, ring - by)]
 
     barrier = pltpu.get_barrier_semaphore()
-    greeted = [up, down] + group_peers + around(1)
+    greeted = [up, down, owners[0], owners[2], workers[0], workers[2]] + group_peers + around(1)
     for peer in greeted:
         signal(barrier, peer)
     for load in loads[2:]:
@@ -188,37 +212,74 @@
     loads[1].wait()
     pad_rows[...] = jnp.zeros_like(pad_rows)
     for r in range(height):
-        pad_rows[r, 0:channels, :] = pixels[:, r, :]
-        pad_rows[height + r, 0:channels, :] = (2 * probes[:, r, :] - 1).astype(jnp.float32)
-    for side in range(2):
-        halo_send[0, side, 0:CH, :] = pad_rows[side].astype(jnp.bfloat16)
-        halo_send[0, side, CH : 2 * CH, :] = pad_rows[2 + side].astype(jnp.bfloat16)
+        pad_rows[2 * r, 0:channels, :] = pixels[:, r, :]
+        pad_rows[2 * r + 1, 0:channels, :] = (2 * probes[:, r, :] - 1).astype(jnp.float32)
+    for k in range(2 * height):
+        slab_send[CH * k : CH * (k + 1), :] = pad_rows[k].astype(jnp.bfloat16)
 
     pl.semaphore_wait(barrier, len(greeted))
 
+    def remote(source, place, sent, arrived, peer):
+        return pltpu.make_async_remote_copy(
+            src_ref=source,
+            dst_ref=place,
+            send_sem=sent,
+            recv_sem=arrived,
+            device_id={"rows": peer},
+            device_id_type=MESH,
+        )
+
     def exchange(send, recv, index):
-        made = []
-        for side, peer in enumerate((up, down)):
-            copy = pltpu.make_async_remote_copy(
-                src_ref=send.at[side],
-                dst_ref=recv.at[1 - side],
-                send_sem=send_sem.at[index, side],
-                recv_sem=recv_sem.at[index, 1 - side],
-                device_id={"rows": peer},
-                device_id_type=MESH,
-            )
+        made = [
+            remote(send.at[side], recv.at[1 - side], send_sem.at[index, side], recv_sem.at[index, 1 - side], peer)
+            for side, peer in enumerate((up, down))
+        ]
+        for copy in made:
             copy.start()
-            made.append(copy)
         return made
 
     def finish(made):
         for copy in made:
             copy.wait()
 
+    def hand_over(sources, places, peers, index):
+        made = [
+            remote(source, place, three_send.at[index, k], three_recv.at[index, k], peer)
+            for k, (source, place, peer) in enumerate(zip(sources, places, peers))
+        ]
+        made[0].start()
+        made[2].start()
+        local = pltpu.make_async_copy(sources[1], places[1], three_recv.at[index, 1])
+
+        @pl.when(jnp.logical_not(stays))
+        def _():
+            made[1].start()
+
+        @pl.when(stays)
+        def _():
+            local.start()
+
+        return made
+
+    def take_over(made):
+        for copy in made:
+            copy.wait_recv()
+        made[0].wait_send()
+        made[2].wait_send()
+
+        @pl.when(jnp.logical_not(stays))
+        def _():
+            made[1].wait_send()
+
     def inside(value, outside):
         return jnp.where(outside, 0.0, value)
 
-    first = exchange(halo_send.at[0], halo_recv.at[0], 0)
+    first = hand_over(
+        (slab_send.at[0 : 2 * CH], slab_send, slab_send.at[2 * CH : 4 * CH]),
+        (slab_below, slab_own, slab_above),
+        workers,
+        0,
+    )
     spread_word(0)
 
     for load in loads[2:]:
@@ -244,10 +305,10 @@
         turned[...] = whole.T[:, :TAPS].astype(jnp.bfloat16)
     mid_turned[...] = mid_weight[...].T
 
-    finish(first)
-    top, bottom = (halo_recv[0, side].astype(jnp.float32) for side in range(2))
-    pix_rows = [inside(top[:CH], is_first), pad_rows[0], pad_rows[1], inside(bottom[:CH], is_last)]
-    signs = [inside(top[CH:], is_first), pad_rows[2], pad_rows[3], inside(bottom[CH:], is_last)]
+    take_over(first)
+    above, own, below = (ref[...].astype(jnp.float32) for ref in (slab_above, slab_own, slab_below))
+    pix_rows = [inside(above[:CH], edges_slab[0]), own[:CH], own[2 * CH : 3 * CH], inside(below[:CH], edges_slab[1])]
+    signs = [inside(above[CH:], edges_slab[0]), own[CH : 2 * CH], own[3 * CH :], inside(below[CH:], edges_slab[1])]
 
     tiles = [slice(at, at + TILE) for at in range(0, height * width, TILE)]
 
@@ -300,13 +361,13 @@
 
     def whole_rows(parts, recv, moving):
         finish(moving)
-        top = inside(recv[0].astype(jnp.float32), is_first)
-        bottom = inside(recv[1].astype(jnp.float32), is_last)
+        top = inside(recv[0].astype(jnp.float32), edges_slab[0])
+        bottom = inside(recv[1].astype(jnp.float32), edges_slab[1])
         return [
-            inside(parts[0], is_first) + top[:CH],
+            inside(parts[0], edges_slab[0]) + top[:CH],
             parts[1] + top[CH:],
             parts[2] + bottom[:CH],
-            inside(parts[3], is_last) + bottom[CH:],
+            inside(parts[3], edges_slab[1]) + bottom[CH:],
         ]
 
     def coefficient(term):
@@ -327,11 +388,14 @@
     for t in tiles:
         taps[:, t] = dot(out_plain[...], act_c[:, t])
     branch = gather_taps(taps, width, False)
-    lat_send[0] = branch[0].astype(jnp.bfloat16)
-    lat_send[1] = branch[3].astype(jnp.bfloat16)
-    lat_moving = exchange(lat_send, lat_recv, TERMS)
+    for r in range(height):
+        lat_own_send[r] = branch[1 + r]
+        lat_send[r] = branch[3 * r].astype(jnp.bfloat16)
+    lat_moving = hand_over(
+        (lat_send.at[0], lat_own_send, lat_send.at[1]), (lat_recv.at[1], lat_own, lat_recv.at[0]), owners, 1
+    )
     pushed_1 = push(signs)
-    pair_moving = send_parts(pushed_1, pair_send, pair_recv, TERMS + 2)
+    pair_moving = send_parts(pushed_1, pair_send, pair_recv, 0)
     hear_word(1)
     spread_word(2)
     vector = whole_rows(parts, halo_recv.at[1], moving)
@@ -339,11 +403,11 @@
     parts = pull_back(vector)
     moving = send_parts(parts, halo_send.at[2], halo_recv.at[2], 2)
     logdet = add_term(logdet, vector, 1)
-    finish(lat_moving)
-    outer = [inside(lat_recv[side].astype(jnp.float32), where) for side, where in enumerate((is_first, is_last))]
+    take_over(lat_moving)
+    outer = [inside(lat_recv[side].astype(jnp.float32), edges_own[side]) for side in range(2)]
     log_prior = []
     for r in range(height):
-        whole = branch[1 + r] + outer[r]
+        whole = lat_own[r] + outer[r]
         latent = pixels[:, r, :] + (whole[:channels] + out_b)
         latent_ref[:, r, :] = latent
         log_prior.append(-0.5 * jnp.sum(latent * latent, axis=0, keepdims=True))
@@ -398,17 +462,19 @@
 
     parts = pull_back(vector)
     dots = [coefficient(4) * jnp.sum(part * sign, axis=0, keepdims=True) for part, sign in zip(parts, signs)]
-    last_send[0] = dots[0]
-    last_send[1] = dots[3]
-    moving = exchange(last_send, last_recv, TERMS + 1)
     logdet = add_term(logdet, vector, 3)
-    known = [log_prior[r] + logdet[r] + dots[1 + r] for r in range(height)]
-    finish(moving)
-    spare = [inside(last_recv[side], where) for side, where in enumerate((is_first, is_last))]
+    for r in range(height):
+        last_send[r] = dots[3 * r]
+        last_own_send[r : r + 1, :] = logdet[r] + dots[1 + r]
+    moving = hand_over(
+        (last_send.at[0], last_own_send, last_send.at[1]), (last_recv.at[1], last_own, last_recv.at[0]), owners, 2
+    )
+    take_over(moving)
+    spare = [inside(last_recv[side], edges_own[side]) for side in range(2)]
     base = 8.0 + 0.5 * math.log(2.0 * math.pi) / math.log(2.0)
     rate = 1.0 / (channels * math.log(2.0))
     for r in range(height):
-        bits_ref[r : r + 1, :] = base - rate * (known[r] + spare[r])
+        bits_ref[r : r + 1, :] = base - rate * (log_prior[r] + (last_own[r : r + 1, :] + spare[r]))
 
     lanes = collect(ring_mine, ring_sums, z, ring_sem, ring)
     mean_ref[0] = base - jnp.sum(lanes) * (rate / (n_rows * height * width))
@@ -432,8 +498,8 @@
         return pl.pallas_call(
             functools.partial(kernel, n_rows, group),
             out_shape=(
-                jax.ShapeDtypeStruct((channels, height, width), f32),
-                jax.ShapeDtypeStruct((height, width), f32),
+                pltpu.VMEM((channels, height, width), f32),
+                pltpu.VMEM((height, width), f32),
                 jax.ShapeDtypeStruct((1,), f32),
             ),
             in_specs=[pl.BlockSpec(memory_space=pltpu.HBM)] * 10,
@@ -465,20 +531,30 @@
                 pltpu.VMEM((hidden, area), bf16),
                 pltpu.VMEM((hidden, area), bf16),
                 pltpu.VMEM((TAPS, area), f32),
+                pltpu.VMEM((4 * CH, width), bf16),
+                pltpu.VMEM((4 * CH, width), bf16),
+                pltpu.VMEM((2 * CH, width), bf16),
+                pltpu.VMEM((2 * CH, width), bf16),
                 pltpu.VMEM((TERMS, 2, 2 * CH, width), bf16),
                 pltpu.VMEM((TERMS, 2, 2 * CH, width), bf16),
                 pltpu.VMEM((2, 2 * CH, width), bf16),
                 pltpu.VMEM((2, 2 * CH, width), bf16),
                 pltpu.VMEM((2, CH, width), bf16),
                 pltpu.VMEM((2, CH, width), bf16),
+                pltpu.VMEM((2, CH, width), f32),
+                pltpu.VMEM((2, CH, width), f32),
                 pltpu.VMEM((2, 1, width), f32),
                 pltpu.VMEM((2, 1, width), f32),
+                pltpu.VMEM((2, width), f32),
+                pltpu.VMEM((2, width), f32),
                 pltpu.VMEM((1, 128), f32),
                 pltpu.VMEM((group, 1, 128), f32),
                 pltpu.VMEM((1, 128), f32),
                 pltpu.VMEM((ring, 1, 128), f32),
-                pltpu.SemaphoreType.DMA((TERMS + 3, 2)),
-                pltpu.SemaphoreType.DMA((TERMS + 3, 2)),
+                pltpu.SemaphoreType.DMA((TERMS, 2)),
+                pltpu.SemaphoreType.DMA((TERMS, 2)),
+                pltpu.SemaphoreType.DMA((3, 3)),
+                pltpu.SemaphoreType.DMA((3, 3)),
                 pltpu.SemaphoreType.DMA((group + ring - 2,)),
                 pltpu.SemaphoreType.DMA((group,)),
                 pltpu.SemaphoreType.DMA((ring,)),

time: 45 us -> 41.9 us (0.931)
  the two profiles are of different devices: /device:TPU:8 before, /device:TPU:1 now
where the time goes in v3:
time: 41.9 us; the launch traced here: 41.7 us
  Pallas kernels  38.1 us (91%)
  between operations  2.33 us (6%)
  local copies, waits for them, and re-layouts  1.21 us (3%)
    pallas_call x1, Pallas kernels, per_device(): pl.pallas_call(functools.partial(kernel, n_rows, group), out_shape=(pltpu...  38.1 us
    unnamed x2, local copies, waits for them, and re-layouts  1.21 us

profile of v3, /device:TPU:1, one launch (start us, length us, event | category | flops | bytes accessed | tf_op | source)
XLA Modules:
  0.0 41.7 jit_solution(1800516040586579098)
XLA Ops:
  0.6 38.1 %shard_map.121 = (f32[12,2,512]{2,1,0:T(2,128)S(1)}, f32[2,512]{1,0:T(2,128)S(1)}, f32[1]{0:T(128)}) custom-call(f32[12,2,512]{2,1,0:T(2,128)} %pixels_hbm.1, s32[12,2,512]{2,1,0:T(2,128)} %probes_hbm.1, bf16[3,3,12,512]{3,2,1,0:T(8,128)(2,1)} %in_weight_hbm.1, f32[1,512]{1,0:T(1,128)} %bitcast.5, f32[1,512]{1,0:T(1,128)} %bitcast.6, ...), custom_call_target="tpu_custom_call" | custom-call | tf_op jit(solution)/shard_map/pallas_call | solution.py:498
  38.8 0.6 %copy.16 = f32[12,2,512]{2,1,0:T(2,128)} copy(f32[12,2,512]{2,1,0:T(2,128)S(1)} %get-tuple-element.3) | data formatting | bytes 98304
  39.4 0.6 %copy.17 = f32[2,512]{1,0:T(2,128)} copy(f32[2,512]{1,0:T(2,128)S(1)} %get-tuple-element.4) | data formatting | bytes 8192

commit v4 on v3

--- a/solution.py
+++ b/solution.py
@@ -17,18 +17,19 @@
 
 def from_left(x):
     lane = lax.broadcasted_iota(jnp.int32, x.shape, 1)
-    return jnp.where(lane == 0, 0.0, pltpu.roll(x, 1, 1))
+    return jnp.where(lane == 0, jnp.zeros_like(x), pltpu.roll(x, 1, 1))
 
 
 def from_right(x):
     last = x.shape[1] - 1
     lane = lax.broadcasted_iota(jnp.int32, x.shape, 1)
-    return jnp.where(lane == last, 0.0, pltpu.roll(x, last, 1))
+    return jnp.where(lane == last, jnp.zeros_like(x), pltpu.roll(x, last, 1))
 
 
 def fill_columns(columns, rows, flipped):
     width = rows[0].shape[1]
     for s, row in enumerate(rows):
+        row = row.astype(jnp.bfloat16)
         for j in range(3):
             if j == 1:
                 piece = row
@@ -36,7 +37,6 @@
                 piece = from_left(row)
             else:
                 piece = from_right(row)
-            piece = piece.astype(jnp.bfloat16)
             for out_row in range(2):
                 i = out_row + 2 - s if flipped else s - out_row
                 if 0 <= i <= 2:
@@ -124,17 +124,16 @@
     last_recv,
     last_own_send,
     last_own,
-    mine,
-    group_sums,
-    ring_mine,
-    ring_sums,
+    pair_mine,
+    pair_sums,
+    chip_mine,
+    chip_sums,
     send_sem,
     recv_sem,
     three_send,
     three_recv,
-    sum_send_sem,
-    group_sem,
-    ring_sem,
+    pair_sem,
+    chip_sem,
     known_sem,
 ):
     channels, height, width = pixels.shape
@@ -143,7 +142,12 @@
     q = lax.rem(me, group)
     z = me // group
     group_peers = [z * group + lax.rem(q + d, group) for d in range(1, group)]
-    ring_peers = [lax.rem(z + d, ring) * group + q for d in range(1, ring)]
+    span = group // 2
+    moves = [(dz, dx) for dz in range(ring) for dx in range(span) if dz or dx]
+    moves.sort(key=lambda m: -(min(m[0], ring - m[0]) + min(m[1], span - m[1])))
+    chip_peers = [
+        lax.rem(z + dz, ring) * group + 2 * lax.rem(q // 2 + dx, span) + lax.rem(q, 2) for dz, dx in moves
+    ]
 
     def worker(slab):
         layer = slab // group
@@ -189,15 +193,17 @@
         return [lax.rem(z + d, ring) * group + q for d in (by, ring - by)]
 
     barrier = pltpu.get_barrier_semaphore()
-    greeted = [up, down, owners[0], owners[2], workers[0], workers[2]] + group_peers + around(1)
+    greeted = [up, down, owners[0], owners[2], workers[0], workers[2]] + group_peers + around(1) + (around(2) if ring > 2 else [])
     for peer in greeted:
         signal(barrier, peer)
     for load in loads[2:]:
         load.start()
 
     steps = []
-    while 2 ** len(steps) < ring // 2:
-        steps.append(2 ** len(steps))
+    reach = 0
+    while reach < ring // 2:
+        steps.append(min(reach + 2, 2 * reach + 1, ring // 2 - reach))
+        reach += steps[-1]
 
     def spread_word(k):
         if k < len(steps):
@@ -324,14 +330,21 @@
         return gate * value, gate * (1.0 + half * (1.0 - t))
 
     fill_columns(columns, pix_rows, False)
-    for t in tiles:
+    def first_layer(t):
         act, slope = lip(dot(in_turned[...], columns[:, t]) + in_b, in_r)
         act_a[:, t] = act.astype(jnp.bfloat16)
         in_slope[:, t] = slope
-    for t in tiles:
+
+    def second_layer(t):
         act, slope = lip(dot(mid_turned[...], act_a[:, t]) + mid_b, mid_r)
         act_c[:, t] = act.astype(jnp.bfloat16)
         mid_slope[:, t] = slope
+
+    first_layer(tiles[0])
+    for before, t in zip(tiles, tiles[1:]):
+        first_layer(t)
+        second_layer(before)
+    second_layer(tiles[-1])
 
     def pull_back(rows):
         fill_columns(columns, rows, True)
@@ -426,38 +439,22 @@
     for at in range(128, width, 128):
         lanes = lanes + total[:, at : at + 128]
 
-    def spread(value, own, slots, slot, others, sems, send_at):
-        own[...] = value
-        made = []
-        for d, peer in enumerate(others):
-            copy = pltpu.make_async_remote_copy(
-                src_ref=own,
-                dst_ref=slots.at[slot],
-                send_sem=sum_send_sem.at[send_at + d],
-                recv_sem=sems.at[slot],
-                device_id={"rows": peer},
-                device_id_type=MESH,
-            )
-            copy.start()
-            made.append(copy)
-        slots[slot] = value
-        return made
-
-    def collect(own, slots, slot, sems, count):
-        for d in range(1, count):
-            other = lax.rem(slot + d, count)
-            pltpu.make_async_copy(own, slots.at[other], sems.at[other]).wait()
-        value = slots[0]
-        for d in range(1, count):
-            value = value + slots[d]
-        return value
-
-    sums = spread(lanes, mine, group_sums, q, group_peers, group_sem, 0)
+    core = lax.rem(me, 2)
+    chip = me // 2
+    pair_mine[...] = lanes
+    pair_sums[core] = lanes
+    pair_copy = remote(pair_mine, pair_sums.at[core], pair_sem.at[0], pair_sem.at[1], me + 1 - 2 * core)
+    pair_copy.start()
+
 
     parts = pull_back(vector)
     moving = send_parts(parts, halo_send.at[3], halo_recv.at[3], 3)
-    lanes = collect(mine, group_sums, q, group_sem, group)
-    sums += spread(lanes, ring_mine, ring_sums, z, ring_peers, ring_sem, group - 1)
+    pair_copy.wait()
+    lanes = pair_sums[0] + pair_sums[1]
+    chip_mine[...] = lanes
+    chip_sums[chip] = lanes
+    for peer in chip_peers:
+        remote(chip_mine, chip_sums.at[chip], chip_sem.at[0], chip_sem.at[1], peer).start()
     vector = whole_rows(parts, halo_recv.at[3], moving)
 
     parts = pull_back(vector)
@@ -476,10 +473,21 @@
     for r in range(height):
         bits_ref[r : r + 1, :] = base - rate * (log_prior[r] + (last_own[r : r + 1, :] + spare[r]))
 
-    lanes = collect(ring_mine, ring_sums, z, ring_sem, ring)
-    mean_ref[0] = base - jnp.sum(lanes) * (rate / (n_rows * height * width))
-    for copy in sums:
-        copy.wait_send()
+    arrived = chip_sums.at[pl.ds(0, n_rows // 2 - 1)]
+    pltpu.make_async_copy(arrived, arrived, chip_sem.at[1]).wait()
+    mean_ref[0] = base - jnp.sum(chip_sums[...]) * (rate / (n_rows * height * width))
+    pltpu.make_async_copy(arrived, arrived, chip_sem.at[0]).wait()
+
+
+def write_out(latent, bits, latent_out, bits_out, sems):
+    copies = [
+        pltpu.make_async_copy(latent, latent_out, sems.at[0]),
+        pltpu.make_async_copy(bits, bits_out, sems.at[1]),
+    ]
+    for copy in copies:
+        copy.start()
+    for copy in copies:
+        copy.wait()
 
 
 def solution(mesh):
@@ -495,7 +503,7 @@
         area = height * width
         f32, bf16 = jnp.float32, jnp.bfloat16
         vmem = pl.BlockSpec(memory_space=pltpu.VMEM)
-        return pl.pallas_call(
+        latent, bits, mean = pl.pallas_call(
             functools.partial(kernel, n_rows, group),
             out_shape=(
                 pltpu.VMEM((channels, height, width), f32),
@@ -548,16 +556,15 @@
                 pltpu.VMEM((2, width), f32),
                 pltpu.VMEM((2, width), f32),
                 pltpu.VMEM((1, 128), f32),
-                pltpu.VMEM((group, 1, 128), f32),
+                pltpu.VMEM((2, 1, 128), f32),
                 pltpu.VMEM((1, 128), f32),
-                pltpu.VMEM((ring, 1, 128), f32),
+                pltpu.VMEM((n_rows // 2, 1, 128), f32),
                 pltpu.SemaphoreType.DMA((TERMS, 2)),
                 pltpu.SemaphoreType.DMA((TERMS, 2)),
                 pltpu.SemaphoreType.DMA((3, 3)),
                 pltpu.SemaphoreType.DMA((3, 3)),
-                pltpu.SemaphoreType.DMA((group + ring - 2,)),
-                pltpu.SemaphoreType.DMA((group,)),
-                pltpu.SemaphoreType.DMA((ring,)),
+                pltpu.SemaphoreType.DMA((2,)),
+                pltpu.SemaphoreType.DMA((2,)),
                 pltpu.SemaphoreType.REGULAR((3,)),
             ],
             compiler_params=pltpu.CompilerParams(
@@ -575,6 +582,19 @@
             out_weight,
             out_bias[None, :],
         )
+        hbm = pl.BlockSpec(memory_space=pltpu.HBM)
+        latent, bits = pl.pallas_call(
+            write_out,
+            out_shape=(
+                jax.ShapeDtypeStruct(latent.shape, f32),
+                jax.ShapeDtypeStruct(bits.shape, f32),
+            ),
+            in_specs=[vmem] * 2,
+            out_specs=(hbm, hbm),
+            scratch_shapes=[pltpu.SemaphoreType.DMA((2,))],
+            compiler_params=pltpu.CompilerParams(vmem_limit_bytes=1024 * 1024),
+        )(latent, bits)
+        return latent, bits, mean
 
     placed = (P("batch", "rows", None),) * 2 + (P(),) * 8
     return jax.shard_map(

time: 41.9 us -> 40.6 us (0.969)
  local copies, waits for them, and re-layouts: 1.21 us -> 0 us
    unnamed x2 -> x0, local copies, waits for them, and re-layouts: 1.21 us -> none
    pallas_call x1, Pallas kernels: 38.1 us -> 37.4 us  [per_device(): pl.pallas_call(functools.partial(kernel, n_rows, group), out_shape=(pltpu...]
    pallas_call x0 -> x1, Pallas kernels: none -> 0.64 us  [per_device(): pl.pallas_call(write_out, out_shape=(jax.ShapeDtypeStruct(latent.shape, f...]
where the time goes in v4:
time: 40.6 us; the launch traced here: 40.4 us
  Pallas kernels  38 us (94%)
  between operations  2.41 us (6%)
    pallas_call x1, Pallas kernels, per_device(): pl.pallas_call(functools.partial(kernel, n_rows, group), out_shape=(pltpu...  37.4 us

profile of v4, /device:TPU:1, one launch (start us, length us, event | category | flops | bytes accessed | tf_op | source)
XLA Modules:
  0.0 40.4 jit_solution(2719903757338475879)
XLA Ops:
  0.6 37.4 %shard_map.121 = (f32[12,2,512]{2,1,0:T(2,128)S(1)}, f32[2,512]{1,0:T(2,128)S(1)}, f32[1]{0:T(128)}) custom-call(f32[12,2,512]{2,1,0:T(2,128)} %pixels_hbm.1, s32[12,2,512]{2,1,0:T(2,128)} %probes_hbm.1, bf16[3,3,12,512]{3,2,1,0:T(8,128)(2,1)} %in_weight_hbm.1, f32[1,512]{1,0:T(1,128)} %bitcast.5, f32[1,512]{1,0:T(1,128)} %bitcast.6, ...), custom_call_target="tpu_custom_call" | custom-call | tf_op jit(solution)/shard_map/pallas_call | solution.py:506
  38.0 0.6 %shard_map.122 = (f32[12,2,512]{2,1,0:T(2,128)}, f32[2,512]{1,0:T(2,128)}) custom-call(f32[12,2,512]{2,1,0:T(2,128)S(1)} %get-tuple-element.8.latent, f32[2,512]{1,0:T(2,128)S(1)} %get-tuple-element.9.bits), custom_call_target="tpu_custom_call" | custom-call | tf_op jit(solution)/shard_map/pallas_call | solution.py:586

commit v5 on v4

--- a/solution.py
+++ b/solution.py
@@ -12,6 +12,7 @@
 CH = 16
 TAPS = 9 * CH
 TILE = 256
+BASE = 8.0 + 0.5 * math.log(2.0 * math.pi) / math.log(2.0)
 MESH = pl.DeviceIdType.MESH
 
 
@@ -81,7 +82,7 @@
     out_bias_hbm,
     latent_ref,
     bits_ref,
-    mean_ref,
+    sum_ref,
     pixels,
     probes,
     in_weight,
@@ -346,12 +347,14 @@
         second_layer(before)
     second_layer(tiles[-1])
 
-    def pull_back(rows):
+    def pull_back(rows, between=None):
         fill_columns(columns, rows, True)
         for t in tiles:
             act_a[:, t] = (dot(out_turned[...], columns[:, t]) * mid_slope[:, t]).astype(jnp.bfloat16)
         for t in tiles:
             act_b[:, t] = (dot(mid_weight[...], act_a[:, t]) * in_slope[:, t]).astype(jnp.bfloat16)
+        if between is not None:
+            between()
         for t in tiles:
             taps[:, t] = dot(in_plain[...], act_b[:, t])
         return gather_taps(taps, width, True)
@@ -447,14 +450,16 @@
     pair_copy.start()
 
 
-    parts = pull_back(vector)
+    def spread_sum():
+        pair_copy.wait()
+        lanes = pair_sums[0] + pair_sums[1]
+        chip_mine[...] = lanes
+        chip_sums[chip] = lanes
+        for peer in chip_peers:
+            remote(chip_mine, chip_sums.at[chip], chip_sem.at[0], chip_sem.at[1], peer).start()
+
+    parts = pull_back(vector, spread_sum)
     moving = send_parts(parts, halo_send.at[3], halo_recv.at[3], 3)
-    pair_copy.wait()
-    lanes = pair_sums[0] + pair_sums[1]
-    chip_mine[...] = lanes
-    chip_sums[chip] = lanes
-    for peer in chip_peers:
-        remote(chip_mine, chip_sums.at[chip], chip_sem.at[0], chip_sem.at[1], peer).start()
     vector = whole_rows(parts, halo_recv.at[3], moving)
 
     parts = pull_back(vector)
@@ -468,24 +473,26 @@
     )
     take_over(moving)
     spare = [inside(last_recv[side], edges_own[side]) for side in range(2)]
-    base = 8.0 + 0.5 * math.log(2.0 * math.pi) / math.log(2.0)
     rate = 1.0 / (channels * math.log(2.0))
     for r in range(height):
-        bits_ref[r : r + 1, :] = base - rate * (log_prior[r] + (last_own[r : r + 1, :] + spare[r]))
+        bits_ref[r : r + 1, :] = BASE - rate * (log_prior[r] + (last_own[r : r + 1, :] + spare[r]))
 
     arrived = chip_sums.at[pl.ds(0, n_rows // 2 - 1)]
     pltpu.make_async_copy(arrived, arrived, chip_sem.at[1]).wait()
-    mean_ref[0] = base - jnp.sum(chip_sums[...]) * (rate / (n_rows * height * width))
+    sum_ref[...] = jnp.sum(chip_sums[...], axis=0)
     pltpu.make_async_copy(arrived, arrived, chip_sem.at[0]).wait()
 
 
-def write_out(latent, bits, latent_out, bits_out, sems):
+def write_out(rate, latent, bits, sums, latent_out, bits_out, mean_out, mean, sems):
     copies = [
         pltpu.make_async_copy(latent, latent_out, sems.at[0]),
         pltpu.make_async_copy(bits, bits_out, sems.at[1]),
     ]
     for copy in copies:
         copy.start()
+    mean[0] = BASE - jnp.sum(sums[...]) * rate
+    copies.append(pltpu.make_async_copy(mean, mean_out, sems.at[2]))
+    copies[2].start()
     for copy in copies:
         copy.wait()
 
@@ -503,15 +510,15 @@
         area = height * width
         f32, bf16 = jnp.float32, jnp.bfloat16
         vmem = pl.BlockSpec(memory_space=pltpu.VMEM)
-        latent, bits, mean = pl.pallas_call(
+        latent, bits, sums = pl.pallas_call(
             functools.partial(kernel, n_rows, group),
             out_shape=(
                 pltpu.VMEM((channels, height, width), f32),
                 pltpu.VMEM((height, width), f32),
-                jax.ShapeDtypeStruct((1,), f32),
+                pltpu.VMEM((1, 128), f32),
             ),
             in_specs=[pl.BlockSpec(memory_space=pltpu.HBM)] * 10,
-            out_specs=(vmem, vmem, pl.BlockSpec(memory_space=pltpu.SMEM)),
+            out_specs=(vmem, vmem, vmem),
             scratch_shapes=[
                 pltpu.VMEM((channels, height, width), f32),
                 pltpu.VMEM((channels, height, width), probes.dtype),
@@ -583,18 +590,19 @@
             out_bias[None, :],
         )
         hbm = pl.BlockSpec(memory_space=pltpu.HBM)
-        latent, bits = pl.pallas_call(
-            write_out,
+        rate = 1.0 / (channels * math.log(2.0) * n_rows * area)
+        return pl.pallas_call(
+            functools.partial(write_out, rate),
             out_shape=(
                 jax.ShapeDtypeStruct(latent.shape, f32),
                 jax.ShapeDtypeStruct(bits.shape, f32),
+                jax.ShapeDtypeStruct((1,), f32),
             ),
-            in_specs=[vmem] * 2,
-            out_specs=(hbm, hbm),
-            scratch_shapes=[pltpu.SemaphoreType.DMA((2,))],
+            in_specs=[vmem] * 3,
+            out_specs=(hbm, hbm, hbm),
+            scratch_shapes=[pltpu.SMEM((1,), f32), pltpu.SemaphoreType.DMA((3,))],
             compiler_params=pltpu.CompilerParams(vmem_limit_bytes=1024 * 1024),
-        )(latent, bits)
-        return latent, bits, mean
+        )(latent, bits, sums)
 
     placed = (P("batch", "rows", None),) * 2 + (P(),) * 8
     return jax.shard_map(

time: 40.6 us -> 37.9 us (0.933)
  between operations: 2.41 us -> 0.64 us
  Pallas kernels: 38 us -> 37.2 us
    pallas_call x1, Pallas kernels: 37.4 us -> 36.5 us  [per_device(): pl.pallas_call(functools.partial(kernel, n_rows, group), out_shape=(pltpu...]
where the time goes in v5:
time: 37.9 us; the launch traced here: 37.8 us
  Pallas kernels  37.2 us (98%)
  between operations  0.64 us (2%)
    pallas_call x1, Pallas kernels, per_device(): pl.pallas_call(functools.partial(kernel, n_rows, group), out_shape=(pltpu...  36.5 us

profile of v5, /device:TPU:1, one launch (start us, length us, event | category | flops | bytes accessed | tf_op | source)
XLA Modules:
  0.0 37.8 jit_solution(7322092427132284588)
XLA Ops:
  0.6 36.5 %shard_map.121 = (f32[12,2,512]{2,1,0:T(2,128)S(1)}, f32[2,512]{1,0:T(2,128)S(1)}, f32[1,128]{1,0:T(1,128)S(1)}) custom-call(f32[12,2,512]{2,1,0:T(2,128)} %pixels_hbm.1, s32[12,2,512]{2,1,0:T(2,128)} %probes_hbm.1, bf16[3,3,12,512]{3,2,1,0:T(8,128)(2,1)} %in_weight_hbm.1, f32[1,512]{1,0:T(1,128)} %bitcast.5, f32[1,512]{1,0:T(1,128)} %bitcast.6, ...), custom_call_target="tpu_custom_call" | custom-call | tf_op jit(solution)/shard_map/pallas_call | solution.py:513
  37.1 0.7 %shard_map.122 = (f32[12,2,512]{2,1,0:T(2,128)}, f32[2,512]{1,0:T(2,128)}, f32[1]{0:T(128)}) custom-call(f32[12,2,512]{2,1,0:T(2,128)S(1)} %get-tuple-element.6.latent, f32[2,512]{1,0:T(2,128)S(1)} %get-tuple-element.7.bits, f32[1,128]{1,0:T(1,128)S(1)} %get-tuple-element.8.sums), custom_call_target="tpu_custom_call" | custom-call | tf_op jit(solution)/shard_map/pallas_call | solution.py:594

commit v6 on v5

--- a/solution.py
+++ b/solution.py
@@ -401,6 +401,8 @@
     moving = send_parts(parts, halo_send.at[1], halo_recv.at[1], 1)
     hear_word(0)
     spread_word(1)
+    pushed_1 = push(signs)
+    pair_moving = send_parts(pushed_1, pair_send, pair_recv, 0)
     for t in tiles:
         taps[:, t] = dot(out_plain[...], act_c[:, t])
     branch = gather_taps(taps, width, False)
@@ -410,8 +412,6 @@
     lat_moving = hand_over(
         (lat_send.at[0], lat_own_send, lat_send.at[1]), (lat_recv.at[1], lat_own, lat_recv.at[0]), owners, 1
     )
-    pushed_1 = push(signs)
-    pair_moving = send_parts(pushed_1, pair_send, pair_recv, 0)
     hear_word(1)
     spread_word(2)
     vector = whole_rows(parts, halo_recv.at[1], moving)
@@ -419,6 +419,7 @@
     parts = pull_back(vector)
     moving = send_parts(parts, halo_send.at[2], halo_recv.at[2], 2)
     logdet = add_term(logdet, vector, 1)
+    pushed_2 = push(whole_rows(pushed_1, pair_recv, pair_moving))
     take_over(lat_moving)
     outer = [inside(lat_recv[side].astype(jnp.float32), edges_own[side]) for side in range(2)]
     log_prior = []
@@ -427,7 +428,6 @@
         latent = pixels[:, r, :] + (whole[:channels] + out_b)
         latent_ref[:, r, :] = latent
         log_prior.append(-0.5 * jnp.sum(latent * latent, axis=0, keepdims=True))
-    pushed_2 = push(whole_rows(pushed_1, pair_recv, pair_moving))
     hear_word(2)
     vector = whole_rows(parts, halo_recv.at[2], moving)
 

time: 37.9 us -> 37.9 us (level)
  no operation moved by 1% of the time
where the time goes in v6:
time: 37.9 us; the launch traced here: 37.8 us
  Pallas kernels  37.1 us (98%)
  between operations  0.64 us (2%)
    pallas_call x1, Pallas kernels, per_device(): pl.pallas_call(functools.partial(kernel, n_rows, group), out_shape=(pltpu...  36.5 us

profile of v6, /device:TPU:1, one launch (start us, length us, event | category | flops | bytes accessed | tf_op | source)
XLA Modules:
  0.0 37.8 jit_solution(4759652538563329772)
XLA Ops:
  0.6 36.5 %shard_map.121 = (f32[12,2,512]{2,1,0:T(2,128)S(1)}, f32[2,512]{1,0:T(2,128)S(1)}, f32[1,128]{1,0:T(1,128)S(1)}) custom-call(f32[12,2,512]{2,1,0:T(2,128)} %pixels_hbm.1, s32[12,2,512]{2,1,0:T(2,128)} %probes_hbm.1, bf16[3,3,12,512]{3,2,1,0:T(8,128)(2,1)} %in_weight_hbm.1, f32[1,512]{1,0:T(1,128)} %bitcast.5, f32[1,512]{1,0:T(1,128)} %bitcast.6, ...), custom_call_target="tpu_custom_call" | custom-call | tf_op jit(solution)/shard_map/pallas_call | solution.py:513
  37.1 0.7 %shard_map.122 = (f32[12,2,512]{2,1,0:T(2,128)}, f32[2,512]{1,0:T(2,128)}, f32[1]{0:T(128)}) custom-call(f32[12,2,512]{2,1,0:T(2,128)S(1)} %get-tuple-element.6.latent, f32[2,512]{1,0:T(2,128)S(1)} %get-tuple-element.7.bits, f32[1,128]{1,0:T(1,128)S(1)} %get-tuple-element.8.sums), custom_call_target="tpu_custom_call" | custom-call | tf_op jit(solution)/shard_map/pallas_call | solution.py:594
